TPU v7x, 128 devices: a whole 4x4x4 slice. The times are simulated.
128 devices in a mesh: inner: 8 (over x, z_hi), cols: 16 (over y, z_lo, core).
Axes of the slice: x: 4, y: 4, z: 4 (z_hi: 2, z_lo: 2; z = z_hi * 2 + z_lo), core: 2. Of those that a mesh axis runs over, the one named last changes fastest.
Arguments:
- x_tiles: float32 [64, 64, 128, 128], P('inner', 'cols'), may hold values from -4 to 4
- tile_col: int32 [64, 64], P('inner', 'cols'), may hold values from 0 to 959, as said below
- keep_mask: int32 [64, 64, 64], P('inner', None, 'cols'), may hold values 0 or 1
- out_rows: int32 [128], P(('inner', 'cols')), may hold values from 0 to 959, as said below
- out_cols: int32 [128], P(('inner', 'cols')), may hold values from 0 to 959, as said below
Outputs:
- product_tiles: float32 [128, 128, 128], P(('inner', 'cols'))
Inputs may be any that keep to these rules, and one draw needn't show every extreme that they name: `tile_col`: within block row k, the 4 entries of column slice c (positions c * 4 to c * 4 + 3) are distinct block columns of c * 60 to c * 60 + 59. `out_cols`: slot s names a block column of column slice (s) % 16 that is stored in some block row. `out_rows`: each slot's block row is stored in some block row together with the slot's block column. The slots of one column slice name block rows that lie in distinct column slices. A slot's two block columns may be stored together in any number of block rows of every index of inner, up to all 8 block rows of one index, and in every draw some slot's are stored together in all 8 block rows of some index.
All inputs are finite; a program needn't handle non-finite values. No bound on the sum of `keep_mask` on one device may be relied on, other than what follows from the above.
Results may differ from a plain program's by a relative error of at most 0.0003.
Values sent between devices are 32-bit elements; how exact they have to be, the bound alone decides.
A program may use at most 128 MiB of HBM per device.

v0:
```python
import jax
import jax.numpy as jnp
from jax import lax
from jax.sharding import PartitionSpec as P


def per_device(x_tiles, tile_col, keep_mask, out_rows, out_cols):
    high = lax.Precision.HIGHEST
    rows_all, cols_all = (
        lax.all_gather(out_rows, "inner", axis=0, tiled=True),
        lax.all_gather(out_cols, "inner", axis=0, tiled=True),
    )
    left = lax.all_gather(x_tiles, "cols", axis=1, tiled=True)
    left_cols = lax.all_gather(tile_col, "cols", axis=1, tiled=True)
    pick_left = (left_cols[None] == rows_all[:, None, None]).astype(jnp.float32)
    keep_part = keep_mask.astype(jnp.float32)
    left_sum = jnp.einsum("mkp,kpab->mkab", pick_left, left, precision=high)
    gate_sum = jnp.einsum("mkp,kpq->mkq", pick_left, keep_part, precision=high)
    pick_right = (tile_col[None] == cols_all[:, None, None]).astype(jnp.float32)
    right_sel = jnp.einsum("mkq,kqab->mkab", gate_sum * pick_right, x_tiles, precision=high)
    partial_value = jnp.einsum("mkab,mkad->mbd", left_sum, right_sel, precision=high)
    return lax.psum_scatter(partial_value, "inner", scatter_dimension=0, tiled=True)


def solution(mesh):
    return jax.shard_map(
        per_device,
        mesh=mesh,
        in_specs=(
            P("inner", "cols", None, None),
            P("inner", "cols"),
            P("inner", None, "cols"),
            P(("inner", "cols")),
            P(("inner", "cols")),
        ),
        out_specs=P(("inner", "cols"), None, None),
        check_vma=False,
    )
```

profile of v0, /device:TPU:1, one launch (start us, length us, event | category | flops | bytes accessed | tf_op | source)
XLA Modules:
  0.0 311.1 jit_solution(16614748856431322377)
XLA Ops:
  6.5 0.0 all-gather.3.cloned.1.call-start
  6.5 0.7 all-gather.3.cloned.1.call-update
  7.3 0.0 reduce-scatter.2.cloned.1.call-start
  8.6 1.2 dynamic-slice
  9.8 0.8 dynamic-update-slice
  10.6 0.8 dynamic-update-slice.1
  11.4 11.8 %all-reduce.2 = (s32[8]{0:T(128)S(1)}, s32[8]{0:T(128)S(1)}) all-reduce(s32[8]{0:T(128)S(1)} %dynamic-update-slice, s32[8]{0:T(128)S(1)} %dynamic-update-slice.1), channel_id=1, replica_groups=mesh['inner'=8,'cols'=16] {'inner'}, use_global_device_ids=true, to_apply=%add | all-reduce | flops 16 | bytes 128
  23.1 0.8 copy.9
  23.9 23.7 %all-gather = s32[16,4,8]{2,1,0:T(4,128)S(1)} all-gather(s32[1,4,8]{2,1,0:T(4,128)} %bitcast.29), channel_id=1, replica_groups=mesh['inner'=8,'cols'=16] {'cols'}, dimensions={0}, use_global_device_ids=true | all-gather | bytes 2176 | tf_op jit(solution)/shard_map/all_gather | solution.py:14
  47.6 0.1 copy.8
  47.7 0.1 fusion.19
  47.7 0.9 fusion.15
  48.6 0.1 copy.14
  48.8 0.1 fusion.13
  48.8 8.4 %fusion.6 = f32[8,8,128,128]{3,1,2,0:T(8,128)} fusion(f32[8,4,128,128]{3,2,1,0:T(8,128)} %param.5, f32[8,8,4,1]{2,1,0,3:T(8,128)S(1)} %fusion.13), kind=kOutput, calls=%fused_computation.6 | convolution fusion | flops 50331648 | bytes 6292480 | tf_op jit(solution)/shard_map/mkq,kqab->mkab/dot_general | solution.py:20
  57.2 126.4 %all-gather.3.cloned.1.call-done = f32[8,64,128,128]{3,2,1,0:T(8,128)} async-done(((f32[8,4,128,128]{3,2,1,0:T(8,128)}), f32[8,64,128,128]{3,2,1,0:T(8,128)}) %all-gather.3.cloned.1.call-update) | async-done | bytes 33554448 | tf_op jit(solution)/shard_map/all_gather | solution.py:13
  183.6 37.4 %fusion = f32[8,8,128,128]{3,1,2,0:T(8,128)} fusion(f32[8,64,128,128]{3,2,1,0:T(8,128)} %all-gather.3.cloned.1.call-done, pred[8,8,64,1]{2,1,0,3:T(8,128)(4,1)S(1)} %get-tuple-element.7), kind=kOutput, calls=%fused_computation | convolution fusion | flops 805306368 | bytes 37752832 | tf_op jit(solution)/shard_map/mkp,kpab->mkab/dot_general | solution.py:17
  221.1 5.4 %copy.12 = f32[8,8,128,128]{2,3,0,1:T(8,128)} copy(f32[8,8,128,128]{3,1,2,0:T(8,128)} %fusion) | data formatting | bytes 8388608 | tf_op jit(solution)/shard_map/mkp,kpab->mkab/dot_general | solution.py:17
  226.4 8.8 %fusion.8 = f32[8,128,128]{2,1,0:T(8,128)} fusion(f32[8,8,128,128]{3,1,2,0:T(8,128)} %fusion.6, f32[8,8,128,128]{2,3,0,1:T(8,128)} %copy.12), kind=kOutput, calls=%fused_computation.8 | convolution fusion | flops 1610612736 | bytes 8912896 | tf_op jit(solution)/shard_map/mkab,mkad->mbd/dot_general | solution.py:21
  235.2 0.0 reduce-scatter.2.cloned.1.call-update
  235.3 69.0 %reduce-scatter.2.cloned.1.call-done = f32[1,128,128]{2,1,0:T(8,128)} async-done(((f32[8,128,128]{2,1,0:T(8,128)}), f32[1,128,128]{2,1,0:T(8,128)}) %reduce-scatter.2.cloned.1.call-update) | async-done | bytes 65552 | tf_op jit(solution)/shard_map/reduce_scatter | solution.py:22
  (2 shorter events, 0.0 us)
Async XLA Ops:
  6.5 177.1 %all-gather.3.cloned.1.call-start = ((), (), s32[]{:S(2)}) async-start(), calls=%async_computation.1 | async-start | bytes 35651584 | tf_op jit(solution)/shard_map/all_gather | solution.py:13
  7.3 297.0 %reduce-scatter.2.cloned.1.call-start = ((), (), s32[]{:S(2)}) async-start(), calls=%async_computation.2 | async-start | bytes 589824 | tf_op jit(solution)/shard_map/reduce_scatter | solution.py:22
Sparse Core Ops, SparseCore 0:
  9.0 174.5 all-gather.2
  235.4 68.8 reduce-scatter.1
where the time goes:
time: 313 us; the launch traced here: 311 us
  waiting for transfers between devices  196 us (63%)
  matrix products  55.5 us (18%)
  blocking collectives  35.5 us (11%)
  between operations  14.7 us (5%)
  local copies, waits for them, and re-layouts  9.09 us (3%)
    all_gather x1, waiting for transfers between devices, per_device(): left = lax.all_gather(x_tiles, 'cols', axis=1, tiled=True)  126 us
    reduce_scatter x1, waiting for transfers between devices, per_device(): lax.psum_scatter(partial_value, 'inner', scatter_dimension=0, tiled=True)  69 us
    dot_general x1, matrix products, per_device(): left_sum = jnp.einsum('mkp,kpab->mkab', pick_left, left, precision=high)  37.4 us
    all_gather x1, blocking collectives, per_device(): left_cols = lax.all_gather(tile_col, 'cols', axis=1, tiled=True)  23.7 us
    unnamed x1, blocking collectives  11.8 us
    dot_general x1, matrix products, per_device(): jnp.einsum('mkab,mkad->mbd', left_sum, right_sel, precision=high)  8.78 us
    dot_general x1, matrix products, per_device(): jnp.einsum('mkq,kqab->mkab', gate_sum * pick_right, x_tiles, precision=high)  8.41 us
  transfers between devices with their start and end apart: 2, of which 2 were waited for; matrix products, arithmetic and copies ran while one was open for 4% of the time, Pallas kernels for 0%

commit v1 on v0

v1 whole, which is shorter than its diff:
```python
import jax
import jax.numpy as jnp
from jax import lax
from jax.experimental import pallas as pl
from jax.experimental.pallas import tpu as pltpu
from jax.sharding import PartitionSpec as P

MESH = pl.DeviceIdType.MESH
JB_DEV = 60
ROWS = 8
AHEAD = 4
LAG = 4
PARTNERS = 15


def kernel(x_hbm, tile_col, keep, out_row, out_col, out, held, right_z, metas, mine, keep_z,
           meta_s, keep_s, weight_l, weight_r, part, part_z, outbox, inbox,
           local_sem, meta_send, meta_recv, y_send, y_recv, f_send, f_recv, z_send, z_recv,
           c_send, c_recv, p_send, p_recv, r_send, r_recv):
    i = lax.axis_index("inner")
    c = lax.axis_index("cols")
    y, z, core = c // 4, (c // 2) % 2, c % 2

    def ring(d, f):
        return (i, ((y + d) % 4) * 4 + z * 2 + (core + f) % 2)

    def inner(e):
        return ((i + e) % 8, c)

    across = (i, y * 4 + (1 - z) * 2 + core)

    def remote(src, dst, send, recv, to):
        return pltpu.make_async_remote_copy(
            src_ref=src, dst_ref=dst, send_sem=send, recv_sem=recv, device_id=to, device_id_type=MESH)

    load_x = pltpu.make_async_copy(x_hbm, held.at[0, pl.ds(0, ROWS)], local_sem.at[0])
    load_x.start()

    lane = lax.broadcasted_iota(jnp.int32, (8, 128), 1)
    mine[...] = jnp.where(lane == 0, out_row[0], jnp.where(lane == 1, out_col[0], 0))
    mine[0:4, 0:8] = tile_col[...]
    metas[0] = mine[...]
    metas[8 + i] = mine[...]
    part[...] = jnp.zeros_like(part)
    part_z[...] = jnp.zeros_like(part_z)

    others = [(d, f) for f in range(2) for d in range(4) if d + f > 0]
    barrier = pltpu.get_barrier_semaphore()
    for d, f in others:
        pl.semaphore_signal(barrier, inc=1, device_id=ring(d, f), device_id_type=MESH)
    for e in range(1, 8):
        pl.semaphore_signal(barrier, inc=1, device_id=inner(e), device_id_type=MESH)
    pl.semaphore_signal(barrier, inc=1, device_id=across, device_id_type=MESH)
    pl.semaphore_wait(barrier, PARTNERS)

    def send_meta():
        copies = []
        for d, f in others:
            n = f * 4 + (4 - d) % 4
            copies.append(remote(mine, metas.at[n], meta_send.at[n], meta_recv.at[n], ring(d, f)))
        for e in range(1, 8):
            copies.append(remote(mine, metas.at[8 + i], meta_send.at[7 + e], meta_recv.at[7 + e], inner(e)))
        copies.append(remote(keep, keep_z, meta_send.at[15], meta_recv.at[15], across))
        return copies

    def own_up(k):
        return remote(held.at[0, k], held.at[0, 24 + k], y_send.at[0, k], y_recv.at[0, k], ring(1, 0))

    def own_down(k):
        return remote(held.at[0, k], held.at[0, 8 + k], y_send.at[1, k], y_recv.at[1, k], ring(3, 0))

    def pass_up(k):
        return remote(held.at[0, 24 + k, pl.ds(0, 2)], held.at[0, 16 + k, pl.ds(0, 2)],
                      f_send.at[0, k], f_recv.at[0, k], ring(1, 0))

    def pass_down(k):
        return remote(held.at[0, 8 + k, pl.ds(2, 2)], held.at[0, 16 + k, pl.ds(2, 2)],
                      f_send.at[1, k], f_recv.at[1, k], ring(3, 0))

    def to_z(k):
        return remote(held.at[0, k], right_z.at[k], z_send.at[k], z_recv.at[k], across)

    def to_core(n):
        return remote(held.at[0, n], held.at[1, n], c_send.at[n], c_recv.at[n], ring(0, 1))

    own_to_core = remote(held.at[0, pl.ds(0, ROWS)], held.at[1, pl.ds(0, ROWS)],
                         c_send.at[0], c_recv.at[0], ring(0, 1))

    def to_reader(a):
        return remote(part_z.at[a], part.at[8 + a], p_send.at[a], p_recv.at[a], across)

    meta = send_meta()
    for copy in meta:
        copy.start()
    load_x.wait()
    for k in range(AHEAD):
        own_up(k).start()
        own_down(k).start()
        to_z(k).start()
    own_to_core.start()

    for copy in meta[7:14]:
        copy.wait_recv()
    meta_z = remote(metas.at[pl.ds(8, 8)], metas.at[pl.ds(16, 8)], meta_send.at[0], meta_recv.at[0], across)
    meta_z.start()
    for copy in meta[:7]:
        copy.wait_recv()
    meta[14].wait_recv()
    meta_z.wait_recv()
    stage = [
        pltpu.make_async_copy(metas, meta_s, local_sem.at[1]),
        pltpu.make_async_copy(keep, keep_s.at[0], local_sem.at[2]),
        pltpu.make_async_copy(keep_z, keep_s.at[1], local_sem.at[3]),
    ]
    for copy in stage:
        copy.start()
    for copy in stage:
        copy.wait()

    def weigh(n, carry):
        h, a = n // 8, n % 8
        holder = ((y + a % 4) % 4) * 4 + z * 2 + (core + a // 4) % 2
        row, col = jnp.int32(-1), jnp.int32(-1)
        for s in range(8):
            r = meta_s[8 + h * 8 + s, 4, 0]
            hit = (r >= holder * JB_DEV) & (r < holder * JB_DEV + JB_DEV)
            row = jnp.where(hit, r, row)
            col = jnp.where(hit, meta_s[8 + h * 8 + s, 4, 1], col)
        reader = h * (16 + i)
        for k in range(ROWS):
            at = (n * ROWS + k) * 4
            left = [(meta_s[a, p, k] == row).astype(jnp.int32) for p in range(4)]
            for p in range(4):
                weight_l[at + p] = left[p].astype(jnp.float32)
            for q in range(4):
                kept = sum(left[p] * keep_s[h, k, q, holder * 4 + p] for p in range(4))
                right = (meta_s[reader, q, k] == col).astype(jnp.int32)
                weight_r[at + q] = (right * kept).astype(jnp.float32)
        return carry

    lax.fori_loop(0, 16, weigh, 0)

    def halves(v):
        top = v.astype(jnp.bfloat16)
        return top, (v - top.astype(jnp.float32)).astype(jnp.bfloat16)

    def add(f, d, k):
        a = f * 4 + d
        for h in range(2):
            at = ((h * 8 + a) * ROWS + k) * 4
            left = sum(weight_l[at + p] * held[f, d * 8 + k, p] for p in range(4))
            if h == 0:
                right = sum(weight_r[at + q] * held[0, k, q] for q in range(4))
            else:
                right = sum(weight_r[at + q] * right_z[k, q] for q in range(4))
            lt, ll = halves(left.T)
            rt, rl = halves(right)
            product = (jnp.dot(lt, rt, preferred_element_type=jnp.float32)
                       + jnp.dot(lt, rl, preferred_element_type=jnp.float32)
                       + jnp.dot(ll, rt, preferred_element_type=jnp.float32))
            if h == 0:
                part[a] += product
            else:
                part_z[a] += product

    own_to_core.wait_recv()

    def step(t, carry):
        @pl.when(t < ROWS)
        def _():
            own_up(t).wait_recv()
            pass_up(t).start()
            to_core(24 + t).start()
            own_down(t).wait_recv()
            pass_down(t).start()
            to_core(8 + t).start()

            @pl.when(t + AHEAD < ROWS)
            def _():
                own_up(t + AHEAD).start()
                own_down(t + AHEAD).start()
                to_z(t + AHEAD).start()

            to_z(t).wait_recv()
            for f, d in ((0, 0), (1, 0), (0, 1), (0, 3)):
                add(f, d, t)

        @pl.when((t >= LAG) & (t < ROWS + LAG))
        def _():
            k = t - LAG
            pass_up(k).wait_recv()
            pass_down(k).wait_recv()
            to_core(16 + k).start()
            add(0, 2, k)

        @pl.when((t >= 1) & (t < ROWS + 1))
        def _():
            k = t - 1
            to_core(24 + k).wait_recv()
            add(1, 3, k)
            to_core(8 + k).wait_recv()
            add(1, 1, k)

        @pl.when(t == ROWS)
        def _():
            for a in (0, 1, 3, 4, 5, 7):
                to_reader(a).start()

        @pl.when(t >= LAG + 1)
        def _():
            k = t - LAG - 1
            to_core(16 + k).wait_recv()
            add(1, 2, k)

        return carry

    lax.fori_loop(0, ROWS + LAG + 1, step, 0)
    for a in (2, 6):
        to_reader(a).start()
    for a in range(8):
        to_reader(a).wait_recv()

    def place(s):
        slice_of = meta_s[8 + s, 4, 0] // JB_DEV
        far = jnp.where((slice_of // 2) % 2 == z, 0, 8)
        other = jnp.where(slice_of % 2 == core, 0, 4)
        return far + other + (slice_of // 4 - y + 4) % 4

    reduce = []
    for e in range(1, 8):
        outbox[e - 1] = part[place((i + e) % 8)]
        copy = remote(outbox.at[e - 1], inbox.at[e - 1], r_send.at[e - 1], r_recv.at[e - 1], inner(e))
        copy.start()
        reduce.append(copy)
    total = part[place(i)]
    for copy in reduce:
        copy.wait_recv()
    for e in range(7):
        total = total + inbox[e]
    out[0] = total

    for copy in meta:
        copy.wait_send()
    meta_z.wait_send()
    own_to_core.wait_send()

    def drain(k, carry):
        own_up(k).wait_send()
        own_down(k).wait_send()
        pass_up(k).wait_send()
        pass_down(k).wait_send()
        to_z(k).wait_send()
        to_core(8 + k).wait_send()
        to_core(16 + k).wait_send()
        to_core(24 + k).wait_send()
        to_reader(k).wait_send()
        return carry

    lax.fori_loop(0, ROWS, drain, 0)
    for copy in reduce:
        copy.wait_send()


def per_device(x_tiles, tile_col, keep_mask, out_rows, out_cols):
    vmem, smem = pltpu.VMEM, pltpu.SMEM
    dma = pltpu.SemaphoreType.DMA
    f32, i32 = jnp.float32, jnp.int32
    return pl.pallas_call(
        kernel,
        out_shape=jax.ShapeDtypeStruct((1, 128, 128), f32),
        in_specs=[
            pl.BlockSpec(memory_space=pl.ANY),
            pl.BlockSpec(memory_space=vmem),
            pl.BlockSpec(memory_space=vmem),
            pl.BlockSpec(memory_space=smem),
            pl.BlockSpec(memory_space=smem),
        ],
        out_specs=pl.BlockSpec(memory_space=vmem),
        scratch_shapes=[
            vmem((2, 32, 4, 128, 128), f32),
            vmem((8, 4, 128, 128), f32),
            vmem((24, 8, 128), i32),
            vmem((8, 128), i32),
            vmem((8, 4, 64), i32),
            smem((24, 8, 128), i32),
            smem((2, 8, 4, 64), i32),
            smem((512,), f32),
            smem((512,), f32),
            vmem((16, 128, 128), f32),
            vmem((8, 128, 128), f32),
            vmem((7, 128, 128), f32),
            vmem((7, 128, 128), f32),
            dma((4,)), dma((16,)), dma((16,)),
            dma((2, 8)), dma((2, 8)), dma((2, 8)), dma((2, 8)),
            dma((8,)), dma((8,)), dma((32,)), dma((32,)),
            dma((8,)), dma((8,)), dma((7,)), dma((7,)),
        ],
        compiler_params=pltpu.CompilerParams(
            collective_id=0, has_side_effects=True, vmem_limit_bytes=40 << 20),
        cost_estimate=pl.CostEstimate(flops=128 * 3 * 2 * 128**3, bytes_accessed=1 << 22, transcendentals=0),
        name="ring_product",
    )(x_tiles, tile_col.T, keep_mask.transpose(0, 2, 1), out_rows, out_cols)


def solution(mesh):
    return jax.shard_map(
        per_device,
        mesh=mesh,
        in_specs=(
            P("inner", "cols", None, None),
            P("inner", "cols"),
            P("inner", None, "cols"),
            P(("inner", "cols")),
            P(("inner", "cols")),
        ),
        out_specs=P(("inner", "cols"), None, None),
        check_vma=False,
    )
```

time: 313 us -> 112 us (0.36)
  waiting for transfers between devices: 196 us -> 0 us
  Pallas kernels: 0 us -> 107 us
  matrix products: 55.5 us -> 0 us
  blocking collectives: 35.5 us -> 0 us
  between operations: 14.7 us -> 1.32 us
  local copies, waits for them, and re-layouts: 9.09 us -> 3.61 us
    all_gather x1 -> x0, waiting for transfers between devices: 126 us -> none  [per_device(): left = lax.all_gather(x_tiles, 'cols', axis=1, tiled=True)]
    pallas_call x0 -> x1, Pallas kernels: none -> 107 us  [per_device(): pl.pallas_call(kernel, out_shape=jax.ShapeDtypeStruct((1, 128, 128), f32)...]
    reduce_scatter x1 -> x0, waiting for transfers between devices: 69 us -> none  [per_device(): lax.psum_scatter(partial_value, 'inner', scatter_dimension=0, tiled=True)]
    dot_general x4 -> x0, matrix products: 55.5 us -> none  [the longest x1 37.4 us: per_device(): left_sum = jnp.einsum('mkp,kpab->mkab', pick_left, left, precision=high)]
    all_gather x1 -> x0, blocking collectives: 23.7 us -> none  [per_device(): left_cols = lax.all_gather(tile_col, 'cols', axis=1, tiled=True)]
    unnamed x1 -> x0, blocking collectives: 11.8 us -> none
    dot_general x2 -> x0, local copies, waits for them, and re-layouts: 5.51 us -> none  [the longest x1 5.38 us: per_device(): left_sum = jnp.einsum('mkp,kpab->mkab', pick_left, left, precision=high)]
  transfers between devices with their start and end apart: 2 -> 0, of which waited for: 2 -> 0; matrix products, arithmetic and copies ran while one was open for 4% -> 0% of each run, Pallas kernels for 0% -> 0%
where the time goes in v1:
time: 112 us
  Pallas kernels  107 us (96%)
  local copies, waits for them, and re-layouts  3.61 us (3%)
  between operations  1.32 us (1%)
    pallas_call x1, Pallas kernels, per_device(): pl.pallas_call(kernel, out_shape=jax.ShapeDtypeStruct((1, 128, 128), f32)...  107 us
    unnamed x7, local copies, waits for them, and re-layouts  3.61 us

profile of v1, /device:TPU:1, one launch (start us, length us, event | category | flops | bytes accessed | tf_op | source)
XLA Modules:
  0.0 112.2 jit_solution(414744910413270595)
XLA Ops:
  1.3 0.0 copy-start
  1.3 1.6 %copy-done = f32[8,4,128,128]{3,2,1,0:T(8,128)S(1)} copy-done((f32[8,4,128,128]{3,2,1,0:T(8,128)S(1)}, f32[8,4,128,128]{3,2,1,0:T(8,128)}, u32[]{:S(2)}) %copy-start) | copy-done | bytes 2097176
  2.9 0.0 copy-start.1
  2.9 0.7 copy-done.1
  3.6 0.0 copy-start.2
  3.6 0.7 copy-done.2
  4.3 107.3 %ring_product.1 = f32[1,128,128]{2,1,0:T(8,128)S(1)} custom-call(f32[8,4,128,128]{3,2,1,0:T(8,128)S(1)} %copy-done, s32[4,8]{1,0:T(4,128)S(1)} %bitcast.3, s32[8,4,64]{2,1,0:T(4,128)S(1)} %bitcast.2, s32[1]{0:T(128)S(6)} %copy.7.out_row, s32[1]{0:T(128)S(6)} %copy.8.out_col), custom_call_target="tpu_custom_call" | custom-call | flops 1610612736 | bytes 4194304 | tf_op jit(solution)/shard_map/ring_product/pallas_call | solution.py:268
  111.6 0.6 copy.9
Async XLA Ops:
  1.3 1.6 %copy-start = (f32[8,4,128,128]{3,2,1,0:T(8,128)S(1)}, f32[8,4,128,128]{3,2,1,0:T(8,128)}, u32[]{:S(2)}) copy-start(f32[8,4,128,128]{3,2,1,0:T(8,128)} %x_hbm.1) | copy-start | bytes 6291460
  2.9 0.7 copy-start.1
  3.6 0.7 copy-start.2

commit v2 on v1

--- a/solution.py
+++ b/solution.py
@@ -13,7 +13,7 @@
 PARTNERS = 15
 
 
-def kernel(x_hbm, tile_col, keep, out_row, out_col, out, held, right_z, metas, mine, keep_z,
+def kernel(x_hbm, tile_col_hbm, keep, out_row, out_col, out, held, right_z, metas, mine, tile_col, keep_z,
            meta_s, keep_s, weight_l, weight_r, part, part_z, outbox, inbox,
            local_sem, meta_send, meta_recv, y_send, y_recv, f_send, f_recv, z_send, z_recv,
            c_send, c_recv, p_send, p_recv, r_send, r_recv):
@@ -35,7 +35,20 @@
 
     load_x = pltpu.make_async_copy(x_hbm, held.at[0, pl.ds(0, ROWS)], local_sem.at[0])
     load_x.start()
-
+    load_col = pltpu.make_async_copy(tile_col_hbm, tile_col, local_sem.at[1])
+    load_col.start()
+    load_keep = pltpu.make_async_copy(keep, keep_s.at[0], local_sem.at[2])
+    load_keep.start()
+
+    others = [(d, f) for f in range(2) for d in range(4) if d + f > 0]
+    barrier = pltpu.get_barrier_semaphore()
+    for d, f in others:
+        pl.semaphore_signal(barrier, inc=1, device_id=ring(d, f), device_id_type=MESH)
+    for e in range(1, 8):
+        pl.semaphore_signal(barrier, inc=1, device_id=inner(e), device_id_type=MESH)
+    pl.semaphore_signal(barrier, inc=1, device_id=across, device_id_type=MESH)
+
+    load_col.wait()
     lane = lax.broadcasted_iota(jnp.int32, (8, 128), 1)
     mine[...] = jnp.where(lane == 0, out_row[0], jnp.where(lane == 1, out_col[0], 0))
     mine[0:4, 0:8] = tile_col[...]
@@ -43,14 +56,6 @@
     metas[8 + i] = mine[...]
     part[...] = jnp.zeros_like(part)
     part_z[...] = jnp.zeros_like(part_z)
-
-    others = [(d, f) for f in range(2) for d in range(4) if d + f > 0]
-    barrier = pltpu.get_barrier_semaphore()
-    for d, f in others:
-        pl.semaphore_signal(barrier, inc=1, device_id=ring(d, f), device_id_type=MESH)
-    for e in range(1, 8):
-        pl.semaphore_signal(barrier, inc=1, device_id=inner(e), device_id_type=MESH)
-    pl.semaphore_signal(barrier, inc=1, device_id=across, device_id_type=MESH)
     pl.semaphore_wait(barrier, PARTNERS)
 
     def send_meta():
@@ -96,26 +101,27 @@
     for k in range(AHEAD):
         own_up(k).start()
         own_down(k).start()
-        to_z(k).start()
     own_to_core.start()
 
     for copy in meta[7:14]:
         copy.wait_recv()
     meta_z = remote(metas.at[pl.ds(8, 8)], metas.at[pl.ds(16, 8)], meta_send.at[0], meta_recv.at[0], across)
     meta_z.start()
+    for k in range(AHEAD):
+        to_z(k).start()
     for copy in meta[:7]:
         copy.wait_recv()
     meta[14].wait_recv()
     meta_z.wait_recv()
     stage = [
         pltpu.make_async_copy(metas, meta_s, local_sem.at[1]),
-        pltpu.make_async_copy(keep, keep_s.at[0], local_sem.at[2]),
         pltpu.make_async_copy(keep_z, keep_s.at[1], local_sem.at[3]),
     ]
     for copy in stage:
         copy.start()
     for copy in stage:
         copy.wait()
+    load_keep.wait()
 
     def weigh(n, carry):
         h, a = n // 8, n % 8
@@ -269,9 +275,9 @@
         kernel,
         out_shape=jax.ShapeDtypeStruct((1, 128, 128), f32),
         in_specs=[
-            pl.BlockSpec(memory_space=pl.ANY),
-            pl.BlockSpec(memory_space=vmem),
-            pl.BlockSpec(memory_space=vmem),
+            pl.BlockSpec(memory_space=pltpu.HBM),
+            pl.BlockSpec(memory_space=pltpu.HBM),
+            pl.BlockSpec(memory_space=pltpu.HBM),
             pl.BlockSpec(memory_space=smem),
             pl.BlockSpec(memory_space=smem),
         ],
@@ -281,6 +287,7 @@
             vmem((8, 4, 128, 128), f32),
             vmem((24, 8, 128), i32),
             vmem((8, 128), i32),
+            vmem((4, 8), i32),
             vmem((8, 4, 64), i32),
             smem((24, 8, 128), i32),
             smem((2, 8, 4, 64), i32),
@@ -296,7 +303,7 @@
             dma((8,)), dma((8,)), dma((7,)), dma((7,)),
         ],
         compiler_params=pltpu.CompilerParams(
-            collective_id=0, has_side_effects=True, vmem_limit_bytes=40 << 20),
+            collective_id=0, has_side_effects=True, vmem_limit_bytes=59 << 20),
         cost_estimate=pl.CostEstimate(flops=128 * 3 * 2 * 128**3, bytes_accessed=1 << 22, transcendentals=0),
         name="ring_product",
     )(x_tiles, tile_col.T, keep_mask.transpose(0, 2, 1), out_rows, out_cols)

time: 112 us -> 97.7 us (0.87)
  Pallas kernels: 107 us -> 94.7 us
  local copies, waits for them, and re-layouts: 3.61 us -> 1.47 us
    pallas_call x1, Pallas kernels: 107 us -> 94.7 us  [per_device(): pl.pallas_call(kernel, out_shape=jax.ShapeDtypeStruct((1, 128, 128), f32)...]
    unnamed x7 -> x1, local copies, waits for them, and re-layouts: 3.61 us -> 1.47 us
where the time goes in v2:
time: 97.7 us; the launch traced here: 97.5 us
  Pallas kernels  94.7 us (97%)
  local copies, waits for them, and re-layouts  1.47 us (2%)
  between operations  1.3 us (1%)
    pallas_call x1, Pallas kernels, per_device(): pl.pallas_call(kernel, out_shape=jax.ShapeDtypeStruct((1, 128, 128), f32)...  94.7 us

profile of v2, /device:TPU:1, one launch (start us, length us, event | category | flops | bytes accessed | tf_op | source)
XLA Modules:
  0.0 97.5 jit_solution(15308024008507223056)
XLA Ops:
  1.3 94.7 %ring_product.1 = f32[1,128,128]{2,1,0:T(8,128)} custom-call(f32[8,4,128,128]{3,2,1,0:T(8,128)} %x_hbm.1, s32[4,8]{1,0:T(4,128)} %bitcast.3, s32[8,4,64]{2,1,0:T(4,128)} %bitcast.2, s32[1]{0:T(128)S(6)} %copy.7.out_row, s32[1]{0:T(128)S(6)} %copy.8.out_col), custom_call_target="tpu_custom_call" | custom-call | flops 1610612736 | bytes 4194304 | tf_op jit(solution)/shard_map/ring_product/pallas_call | solution.py:274
  96.0 1.5 %copy.9 = f32[1,128,128]{2,1,0:T(8,128)} copy(f32[1,128,128]{2,1,0:T(8,128)} %ring_product.1) | data formatting | bytes 131072

commit v3 on v2

v3 whole, which is shorter than its diff:
```python
import jax
import jax.numpy as jnp
from jax import lax
from jax.experimental import pallas as pl
from jax.experimental.pallas import tpu as pltpu
from jax.sharding import PartitionSpec as P

MESH = pl.DeviceIdType.MESH
JB_DEV = 60
ROWS = 8
AHEAD = 8
LAG = 8
PARTNERS = 17


def kernel(x_hbm, tile_col_hbm, keep, out_row, out_col, out, held, right_z, passed, picked, metas, mine, tile_col,
           keeps, meta_s, keep_s, weight_l, weight_r, part, part_z, between, outbox, inbox,
           local_sem, meta_send, meta_recv, list_send, list_recv, y_send, y_recv, f_send, f_recv, z_send, z_recv,
           c_send, c_recv, p_send, p_recv, b_send, b_recv, r_send, r_recv):
    i = lax.axis_index("inner")
    c = lax.axis_index("cols")
    y, z, core = c // 4, (c // 2) % 2, c % 2

    def ring(d, f):
        return (i, ((y + d) % 4) * 4 + z * 2 + (core + f) % 2)

    def inner(e):
        return ((i + e) % 8, c)

    def over_y(d, on):
        return (i, ((y + d) % 4) * 4 + z * 2 + on)

    def over(d, on):
        return (i, ((y + d) % 4) * 4 + (1 - z) * 2 + on)

    across = over(0, core)

    def remote(src, dst, send, recv, to):
        return pltpu.make_async_remote_copy(
            src_ref=src, dst_ref=dst, send_sem=send, recv_sem=recv, device_id=to, device_id_type=MESH)

    load_x = pltpu.make_async_copy(x_hbm, held.at[0, pl.ds(0, ROWS)], local_sem.at[0])
    load_x.start()
    load_col = pltpu.make_async_copy(tile_col_hbm, tile_col, local_sem.at[1])
    load_col.start()
    load_keep = pltpu.make_async_copy(keep, keeps.at[0], local_sem.at[2])
    load_keep.start()

    others = [(d, f) for f in range(2) for d in range(4) if d + f > 0]
    barrier = pltpu.get_barrier_semaphore()
    for d, f in others:
        pl.semaphore_signal(barrier, inc=1, device_id=ring(d, f), device_id_type=MESH)
    for e in range(1, 8):
        pl.semaphore_signal(barrier, inc=1, device_id=inner(e), device_id_type=MESH)
    for to in (across, over(1, 0), over(3, 1)):
        pl.semaphore_signal(barrier, inc=1, device_id=to, device_id_type=MESH)

    load_col.wait()
    lane = lax.broadcasted_iota(jnp.int32, (8, 128), 1)
    mine[...] = jnp.where(lane == 0, out_row[0], jnp.where(lane == 1, out_col[0], 0))
    mine[0:4, 0:8] = tile_col[...]
    metas[0] = mine[...]
    metas[8 + i] = mine[...]
    part[...] = jnp.zeros_like(part)
    part_z[...] = jnp.zeros_like(part_z)
    between[...] = jnp.zeros_like(between)
    pl.semaphore_wait(barrier, PARTNERS)

    slots = [remote(mine, metas.at[8 + i], meta_send.at[7 + e], meta_recv.at[7 + e], inner(e)) for e in range(1, 8)]
    holders = []
    for d, f in others:
        n = f * 4 + (4 - d) % 4
        holders.append(remote(mine, metas.at[n], meta_send.at[n], meta_recv.at[n], ring(d, f)))

    def lists(h, to):
        return remote(metas.at[pl.ds(8, 8)], metas.at[pl.ds(8 + 8 * h, 8)], list_send.at[h], list_recv.at[h], to)

    def filters(h, to):
        return remote(keep, keeps.at[h], list_send.at[5 + h], list_recv.at[5 + h], to)

    filter_copies = [filters(1, across), filters(2, ring(3, 0)), filters(3, ring(1, 0))]
    list_copies = [lists(1, across), lists(2, ring(3, 0)), lists(3, ring(1, 0))]

    def diagonal(on):
        h = 4 + core
        return remote(metas.at[pl.ds(8, 8)], metas.at[pl.ds(8 + 8 * h, 8)], list_send.at[9 + on], list_recv.at[h],
                      over(3 + 2 * core, on))

    diagonal_copies = [diagonal(0), diagonal(1)]

    def own_up(k):
        return remote(held.at[0, k], held.at[0, 24 + k], y_send.at[0, k], y_recv.at[0, k], ring(1, 0))

    def own_down(k):
        return remote(held.at[0, k], held.at[0, 8 + k], y_send.at[1, k], y_recv.at[1, k], ring(3, 0))

    def pass_up(k):
        return remote(picked.at[0, k], passed.at[core, k], f_send.at[0, k], f_recv.at[core, k], over_y(1, 0))

    def pass_down(k):
        return remote(picked.at[1, k], passed.at[1 - core, k], f_send.at[1, k], f_recv.at[1 - core, k], over_y(3, 1))

    def arrived(f, k):
        return remote(picked.at[f, k], passed.at[f, k], f_send.at[f, k], f_recv.at[f, k], over_y(1, 0))

    def to_z(k):
        return remote(held.at[0, k], right_z.at[k], z_send.at[k], z_recv.at[k], across)

    def to_core(n):
        return remote(held.at[0, n], held.at[1, n], c_send.at[n], c_recv.at[n], ring(0, 1))

    own_to_core = remote(held.at[0, pl.ds(0, ROWS)], held.at[1, pl.ds(0, ROWS)],
                         c_send.at[0], c_recv.at[0], ring(0, 1))

    def to_reader(a):
        return remote(part_z.at[a], part.at[8 + a], p_send.at[a], p_recv.at[a], across)

    back_up = remote(between.at[0], part.at[2], b_send.at[0], b_recv.at[0], ring(1, 0))
    back_down = remote(between.at[1], part.at[6], b_send.at[1], b_recv.at[1], ring(3, 0))

    def start_rows(k):
        own_up(k).start()
        own_down(k).start()
        to_z(k).start()

    for copy in slots:
        copy.start()
    load_x.wait()
    start_rows(0)
    for copy in holders + filter_copies:
        copy.start()
    for copy in slots:
        copy.wait_recv()
    for copy in list_copies + diagonal_copies:
        copy.start()
    for k in range(1, AHEAD):
        start_rows(k)
    own_to_core.start()
    for copy in holders + filter_copies + list_copies:
        copy.wait_recv()
    for h in (4, 5):
        remote(metas.at[pl.ds(8, 8)], metas.at[pl.ds(8 + 8 * h, 8)], list_send.at[5 + h], list_recv.at[h], across).wait_recv()
    load_keep.wait()
    stage = [
        pltpu.make_async_copy(metas, meta_s, local_sem.at[1]),
        pltpu.make_async_copy(keeps, keep_s, local_sem.at[3]),
    ]
    for copy in stage:
        copy.start()
    for copy in stage:
        copy.wait()

    def weigh(n, carry):
        h = jnp.where(n < 16, n // 8, n - 14)
        a = jnp.where(n < 16, n % 8, jnp.where(n == 17, 5, jnp.where(n == 19, 1, 3)))
        holder = ((y + a % 4) % 4) * 4 + z * 2 + (core + a // 4) % 2
        row, col = jnp.int32(-1), jnp.int32(-1)
        for s in range(8):
            r = meta_s[8 + h * 8 + s, 4, 0]
            hit = (r >= holder * JB_DEV) & (r < holder * JB_DEV + JB_DEV)
            row = jnp.where(hit, r, row)
            col = jnp.where(hit, meta_s[8 + h * 8 + s, 4, 1], col)
        reader = 8 + h * 8 + i
        filter_of = jnp.minimum(h, 3)
        for k in range(ROWS):
            at = (n * ROWS + k) * 4
            left = [(meta_s[a, p, k] == row).astype(jnp.int32) for p in range(4)]
            for p in range(4):
                weight_l[at + p] = left[p].astype(jnp.float32)
            for q in range(4):
                kept = sum(left[p] * keep_s[filter_of, k, q, holder * 4 + p] for p in range(4))
                right = (meta_s[reader, q, k] == col).astype(jnp.int32)
                weight_r[at + q] = (right * kept).astype(jnp.float32)
        return carry

    lax.fori_loop(0, 20, weigh, 0)

    def halves(v):
        top = v.astype(jnp.bfloat16)
        return top, (v - top.astype(jnp.float32)).astype(jnp.bfloat16)

    def choose(weights, n, k, row):
        at = (n * ROWS + k) * 4
        return sum(weights[at + p] * row[p] for p in range(4))

    def multiply(left, right):
        lt, ll = halves(left.T)
        rt, rl = halves(right)
        return (jnp.dot(lt, rt, preferred_element_type=jnp.float32)
                + jnp.dot(lt, rl, preferred_element_type=jnp.float32)
                + jnp.dot(ll, rt, preferred_element_type=jnp.float32))

    def add(f, d, k):
        a = f * 4 + d
        row = held.at[f, d * 8 + k]
        part[a] += multiply(choose(weight_l, a, k, row), choose(weight_r, a, k, held.at[0, k]))
        part_z[a] += multiply(choose(weight_l, 8 + a, k, row), choose(weight_r, 8 + a, k, right_z.at[k]))

    def add_passed(f, k):
        a = f * 4 + 2
        part_z[a] += multiply(passed[f, k], choose(weight_r, 8 + a, k, right_z.at[k]))

    def add_between(g, k):
        left = held.at[0, 24 + k] if g == 0 else held.at[1, 8 + k]
        right = held.at[0, 8 + k] if g == 0 else held.at[0, 24 + k]
        between[g] += multiply(choose(weight_l, 16 + g, k, left), choose(weight_r, 16 + g, k, right))

    own_to_core.wait_recv()

    def step(t, carry):
        @pl.when(t < ROWS)
        def _():
            own_up(t).wait_recv()
            picked[0, t] = choose(weight_l, 18, t, held.at[0, 24 + t])
            pass_up(t).start()
            to_core(24 + t).start()
            own_down(t).wait_recv()
            picked[1, t] = choose(weight_l, 19, t, held.at[0, 8 + t])
            pass_down(t).start()
            to_core(8 + t).start()

            @pl.when(t + AHEAD < ROWS)
            def _():
                start_rows(t + AHEAD)

            to_z(t).wait_recv()
            for f, d in ((0, 0), (1, 0), (0, 1), (0, 3)):
                add(f, d, t)
            add_between(0, t)

        @pl.when((t >= 1) & (t < ROWS + 1))
        def _():
            k = t - 1
            to_core(8 + k).wait_recv()
            add(1, 1, k)
            add_between(1, k)
            to_core(24 + k).wait_recv()
            add(1, 3, k)

        @pl.when(t == ROWS)
        def _():
            for a in (0, 1, 3, 4, 5, 7):
                to_reader(a).start()
            back_up.start()
            back_down.start()

        @pl.when(t >= LAG)
        def _():
            k = t - LAG
            for f in range(2):
                arrived(f, k).wait_recv()
                add_passed(f, k)

        return carry

    lax.fori_loop(0, ROWS + LAG, step, 0)
    for a in (2, 6):
        to_reader(a).start()
    for a in range(8):
        to_reader(a).wait_recv()
    back_up.wait_recv()
    back_down.wait_recv()

    def place(s):
        slice_of = meta_s[8 + s, 4, 0] // JB_DEV
        far = jnp.where((slice_of // 2) % 2 == z, 0, 8)
        other = jnp.where(slice_of % 2 == core, 0, 4)
        return far + other + (slice_of // 4 - y + 4) % 4

    reduce = []
    for e in range(1, 8):
        outbox[e - 1] = part[place((i + e) % 8)]
        copy = remote(outbox.at[e - 1], inbox.at[e - 1], r_send.at[e - 1], r_recv.at[e - 1], inner(e))
        copy.start()
        reduce.append(copy)
    total = part[place(i)]
    for copy in reduce:
        copy.wait_recv()
    for e in range(7):
        total = total + inbox[e]
    out[0] = total

    for copy in slots + holders + filter_copies + list_copies + diagonal_copies + [own_to_core, back_up, back_down]:
        copy.wait_send()

    def drain(k, carry):
        own_up(k).wait_send()
        own_down(k).wait_send()
        pass_up(k).wait_send()
        pass_down(k).wait_send()
        to_z(k).wait_send()
        to_core(8 + k).wait_send()
        to_core(24 + k).wait_send()
        to_reader(k).wait_send()
        return carry

    lax.fori_loop(0, ROWS, drain, 0)
    for copy in reduce:
        copy.wait_send()


def per_device(x_tiles, tile_col, keep_mask, out_rows, out_cols):
    vmem, smem = pltpu.VMEM, pltpu.SMEM
    dma = pltpu.SemaphoreType.DMA
    f32, i32 = jnp.float32, jnp.int32
    return pl.pallas_call(
        kernel,
        out_shape=jax.ShapeDtypeStruct((1, 128, 128), f32),
        in_specs=[
            pl.BlockSpec(memory_space=pltpu.HBM),
            pl.BlockSpec(memory_space=pltpu.HBM),
            pl.BlockSpec(memory_space=pltpu.HBM),
            pl.BlockSpec(memory_space=smem),
            pl.BlockSpec(memory_space=smem),
        ],
        out_specs=pl.BlockSpec(memory_space=vmem),
        scratch_shapes=[
            vmem((2, 32, 4, 128, 128), f32),
            vmem((8, 4, 128, 128), f32),
            vmem((2, 8, 128, 128), f32),
            vmem((2, 8, 128, 128), f32),
            vmem((56, 8, 128), i32),
            vmem((8, 128), i32),
            vmem((4, 8), i32),
            vmem((4, 8, 4, 64), i32),
            smem((56, 8, 128), i32),
            smem((4, 8, 4, 64), i32),
            smem((640,), f32),
            smem((640,), f32),
            vmem((16, 128, 128), f32),
            vmem((8, 128, 128), f32),
            vmem((2, 128, 128), f32),
            vmem((7, 128, 128), f32),
            vmem((7, 128, 128), f32),
            dma((4,)), dma((16,)), dma((16,)), dma((11,)), dma((11,)),
            dma((2, 8)), dma((2, 8)), dma((2, 8)), dma((2, 8)),
            dma((8,)), dma((8,)), dma((32,)), dma((32,)),
            dma((8,)), dma((8,)), dma((2,)), dma((2,)), dma((7,)), dma((7,)),
        ],
        compiler_params=pltpu.CompilerParams(
            collective_id=0, has_side_effects=True, vmem_limit_bytes=59 << 20),
        cost_estimate=pl.CostEstimate(flops=128 * 3 * 2 * 128**3, bytes_accessed=1 << 22, transcendentals=0),
        name="ring_product",
    )(x_tiles, tile_col.T, keep_mask.transpose(0, 2, 1), out_rows, out_cols)


def solution(mesh):
    return jax.shard_map(
        per_device,
        mesh=mesh,
        in_specs=(
            P("inner", "cols", None, None),
            P("inner", "cols"),
            P("inner", None, "cols"),
            P(("inner", "cols")),
            P(("inner", "cols")),
        ),
        out_specs=P(("inner", "cols"), None, None),
        check_vma=False,
    )
```

time: 97.7 us -> 87.2 us (0.89)
  Pallas kernels: 94.7 us -> 83.4 us
    pallas_call x1, Pallas kernels: 94.7 us -> 83.4 us  [per_device(): pl.pallas_call(kernel, out_shape=jax.ShapeDtypeStruct((1, 128, 128), f32)...]
where the time goes in v3:
time: 87.2 us; the launch traced here: 86.1 us
  Pallas kernels  83.4 us (96%)
  local copies, waits for them, and re-layouts  1.47 us (2%)
  between operations  1.3 us (1%)
    pallas_call x1, Pallas kernels, per_device(): pl.pallas_call(kernel, out_shape=jax.ShapeDtypeStruct((1, 128, 128), f32)...  83.4 us

profile of v3, /device:TPU:1, one launch (start us, length us, event | category | flops | bytes accessed | tf_op | source)
XLA Modules:
  0.0 86.1 jit_solution(11651075464314940525)
XLA Ops:
  1.3 83.4 %ring_product.1 = f32[1,128,128]{2,1,0:T(8,128)} custom-call(f32[8,4,128,128]{3,2,1,0:T(8,128)} %x_hbm.1, s32[4,8]{1,0:T(4,128)} %bitcast.3, s32[8,4,64]{2,1,0:T(4,128)} %bitcast.2, s32[1]{0:T(128)S(6)} %copy.7.out_row, s32[1]{0:T(128)S(6)} %copy.8.out_col), custom_call_target="tpu_custom_call" | custom-call | flops 1610612736 | bytes 4194304 | tf_op jit(solution)/shard_map/ring_product/pallas_call | solution.py:306
  84.7 1.5 %copy.9 = f32[1,128,128]{2,1,0:T(8,128)} copy(f32[1,128,128]{2,1,0:T(8,128)} %ring_product.1) | data formatting | bytes 131072

commit v4 on v0

v4 whole, which is shorter than its diff:
```python
import jax
import jax.numpy as jnp
from jax import lax
from jax.experimental import pallas as pl
from jax.experimental.pallas import tpu as pltpu
from jax.sharding import PartitionSpec as P

MESH = pl.DeviceIdType.MESH
JB_DEV = 60
PARTNERS = 16
STEPS = ((2, 1), (1, 1), (3, 1), (2, 0), (1, 0), (3, 0), (0, 1))
PARTS = ((0, 48, (0, 1, 2)), (48, 40, (1, 2, 0)), (88, 40, (2, 0, 1)))


def kernel(x, tile_col_hbm, keep_hbm, out_row, out_col, out, held, products, tile_col, keep, mine, slots, notes, heard,
           heard_s, left_s, right_s, gate_s, one_a, one_b, one_c, two_a, two_b, two_c, three_a, three_b, three_c,
           sum_a, sum_b, sum_c, line_a, line_b, line_c,
           local_sem, s_send, s_recv, n_send, n_recv, g_send, g_recv, c_send, c_recv, h_send, h_recv, r_send, r_recv):
    i = lax.axis_index("inner")
    c = lax.axis_index("cols")
    core = c % 2
    at = (i // 2, c // 4, (i % 2) * 2 + (c // 2) % 2)
    z_hi, z_lo = i % 2, (c // 2) % 2
    home = at[1] * 2 + z_lo

    def device(place, on):
        px, py, pz = place
        return (px * 2 + pz // 2, py * 4 + (pz % 2) * 2 + on)

    def row_home(step):
        py, pz = (at[1] + step[0]) % 4, (z_lo + step[1]) % 2
        return py * 2 + pz, device((at[0], py, z_hi * 2 + pz), core)

    def inner(e):
        return ((i + e) % 8, c)

    def along(axis, d):
        return device(tuple((p + d) % 4 if n == axis else p for n, p in enumerate(at)), core)

    twin = device(at, 1 - core)

    def remote(src, dst, send, recv, to):
        return pltpu.make_async_remote_copy(
            src_ref=src, dst_ref=dst, send_sem=send, recv_sem=recv, device_id=to, device_id_type=MESH)

    load_col = pltpu.make_async_copy(tile_col_hbm, tile_col, local_sem.at[0])
    load_keep = pltpu.make_async_copy(keep_hbm, keep, local_sem.at[1])
    load_own = pltpu.make_async_copy(x.at[home], held.at[pl.ds(home * 4, 4)], local_sem.at[2])
    load_col.start()
    load_keep.start()
    load_own.start()

    barrier = pltpu.get_barrier_semaphore()
    partners = [row_home(step)[1] for step in STEPS] + [inner(e) for e in range(1, 8)]
    partners += [twin, device((at[0], at[1], 3 - at[2]), core)]
    for to in partners:
        pl.semaphore_signal(barrier, inc=1, device_id=to, device_id_type=MESH)

    sublane = lax.broadcasted_iota(jnp.int32, (8, 128), 0)
    lane = lax.broadcasted_iota(jnp.int32, (8, 128), 1)
    mine[...] = jnp.where(sublane == 4, out_row[0], jnp.where(sublane == 5, out_col[0], 0))
    slots[i] = mine[...]
    load_col.wait()
    load_keep.wait()
    pl.semaphore_wait(barrier, PARTNERS)

    slot_copies = [remote(mine, slots.at[i], s_send.at[e - 1], s_recv.at[e - 1], inner(e)) for e in range(1, 8)]
    for copy in slot_copies:
        copy.start()

    def send_blocks(p):
        for j, step in enumerate(STEPS):
            row, to = row_home(step)
            remote(x.at[row, p], held.at[home * 4 + p], g_send.at[j], g_recv.at[home], to).start()

    send_blocks(0)
    for copy in slot_copies:
        copy.wait_recv()

    listed = jnp.zeros((8, 128), jnp.int32)
    for s in range(8):
        listed = jnp.where(lane == s, slots[s], listed)
    for k in range(8):
        notes[k] = listed
        notes[k, 0:4, 0:64] = keep[k]
        notes[k, 0:4, 64:128] = jnp.broadcast_to(tile_col[:, k:k + 1], (4, 64))
    heard[home] = notes[home]

    def note(j):
        row, to = row_home(STEPS[j])
        return remote(notes.at[row], heard.at[home], n_send.at[j], n_recv.at[home], to)

    for j in range(7):
        note(j).start()
    for p in range(1, 4):
        send_blocks(p)

    def from_chip(step):
        source, to = row_home(step)
        return source, remote(notes.at[0], heard.at[source], n_send.at[0], n_recv.at[source], to), remote(
            held.at[pl.ds(0, 4)], held.at[pl.ds(source * 4, 4)], g_send.at[0], g_recv.at[source], to)

    for step in STEPS:
        from_chip(step)[1].wait_recv()
    share_notes = remote(heard.at[pl.ds(0, 8)], heard.at[pl.ds(8, 8)], h_send.at[0], h_recv.at[0], twin)
    share_notes.start()

    def share(source):
        return remote(held.at[pl.ds(source * 4, 4)], held.at[pl.ds(32 + source * 4, 4)],
                      c_send.at[source], c_recv.at[source], twin)

    load_own.wait()
    share(home).start()
    share_notes.wait_recv()
    stage = pltpu.make_async_copy(heard, heard_s, local_sem.at[3])
    stage.start()
    stage.wait()

    def find(n, carry):
        sx, sy, sz = n // 16, (n // 4) % 4, n % 4
        index, chip = sx * 2 + sz // 2, sy * 2 + sz % 2
        row, col = heard_s[chip, 4, index], heard_s[chip, 5, index]
        left_slice = row // JB_DEV
        holder = jnp.where(left_slice % 2 == core, 0, 8) + left_slice // 2
        p, q, stored_l, stored_r = jnp.int32(0), jnp.int32(0), jnp.int32(0), jnp.int32(0)
        for r in range(4):
            hit = heard_s[holder, r, 64] == row
            p, stored_l = jnp.where(hit, r, p), jnp.where(hit, 1, stored_l)
            hit = heard_s[chip, r, 64] == col
            q, stored_r = jnp.where(hit, r, q), jnp.where(hit, 1, stored_r)
        left_s[n] = holder * 4 + p
        right_s[n] = chip * 4 + q
        gate_s[n] = (heard_s[chip, q, left_slice * 4 + p] * stored_l * stored_r).astype(jnp.float32)
        return carry

    lax.fori_loop(0, 64, find, 0)

    for step in STEPS[::-1]:
        source, _, blocks = from_chip(step)
        blocks.wait_recv()
        share(source).start()
    for source in range(8):
        share(source).wait_recv()

    def halves(v):
        top = v.astype(jnp.bfloat16)
        return top, (v - top.astype(jnp.float32)).astype(jnp.bfloat16)

    def product(n):
        lt, ll = halves(held[left_s[n]].T)
        rt, rl = halves(held[right_s[n]] * gate_s[n])
        return (jnp.dot(lt, rt, preferred_element_type=jnp.float32)
                + jnp.dot(lt, rl, preferred_element_type=jnp.float32)
                + jnp.dot(ll, rt, preferred_element_type=jnp.float32))

    ones, twos, threes = (one_a, one_b, one_c), (two_a, two_b, two_c), (three_a, three_b, three_c)
    sums, lines = (sum_a, sum_b, sum_c), (line_a, line_b, line_c)

    def pick(axes_left, axis, where):
        return tuple(where if a == axis else slice(None) for a in axes_left)

    def first(part, d):
        start, rows, (axis, _, _) = PARTS[part]
        cut = pick((0, 1, 2), axis, (at[axis] + d) % 4) + (pl.ds(start, rows),)
        return remote(products.at[cut], ones[part].at[d - 1], r_send.at[part, d - 1], r_recv.at[part, d - 1], along(axis, d))

    def second(part, d):
        _, _, (gone, axis, _) = PARTS[part]
        cut = pick([a for a in range(3) if a != gone], axis, (at[axis] + d) % 4)
        return remote(sums[part].at[cut], twos[part].at[d - 1], r_send.at[part, 2 + d], r_recv.at[part, 2 + d], along(axis, d))

    def third(part, d):
        _, _, (_, _, axis) = PARTS[part]
        return remote(lines[part].at[(at[axis] + d) % 4], threes[part].at[d - 1],
                      r_send.at[part, 5 + d], r_recv.at[part, 5 + d], along(axis, d))

    def slab(px):
        def body(n, carry):
            products[px, n // 4, n % 4] = product(px * 16 + n)
            return carry

        lax.fori_loop(0, 16, body, 0)

    for d in (2, 1, 3):
        slab((at[0] + d) % 4)
        first(0, d).start()
    slab(at[0])
    for d in (2, 1, 3):
        for part in (1, 2):
            first(part, d).start()

    for part, (start, rows, (axis, _, _)) in enumerate(PARTS):
        for d in range(1, 4):
            first(part, d).wait_recv()
        cut = pick((0, 1, 2), axis, at[axis]) + (pl.ds(start, rows),)
        sums[part][...] = products[cut] + ones[part][0] + ones[part][1] + ones[part][2]
        for d in (2, 1, 3):
            second(part, d).start()
    for part, (_, _, (gone, axis, _)) in enumerate(PARTS):
        for d in range(1, 4):
            second(part, d).wait_recv()
        cut = pick([a for a in range(3) if a != gone], axis, at[axis])
        lines[part][...] = sums[part][cut] + twos[part][0] + twos[part][1] + twos[part][2]
        for d in (2, 1, 3):
            third(part, d).start()
    for part, (start, rows, (_, _, axis)) in enumerate(PARTS):
        for d in range(1, 4):
            third(part, d).wait_recv()
        out[0, pl.ds(start, rows)] = lines[part][at[axis]] + threes[part][0] + threes[part][1] + threes[part][2]

    for copy in slot_copies + [share_notes]:
        copy.wait_send()
    for j, step in enumerate(STEPS):
        note(j).wait_send()
        row, to = row_home(step)
        remote(x.at[row], held.at[pl.ds(home * 4, 4)], g_send.at[j], g_recv.at[home], to).wait_send()
    for source in range(8):
        share(source).wait_send()
    for part in range(3):
        for d in range(1, 4):
            first(part, d).wait_send()
            second(part, d).wait_send()
            third(part, d).wait_send()


def per_device(x_tiles, tile_col, keep_mask, out_rows, out_cols):
    vmem, smem = pltpu.VMEM, pltpu.SMEM
    dma = pltpu.SemaphoreType.DMA
    f32, i32 = jnp.float32, jnp.int32
    rows = [part[1] for part in PARTS]
    return pl.pallas_call(
        kernel,
        out_shape=jax.ShapeDtypeStruct((1, 128, 128), f32),
        in_specs=[
            pl.BlockSpec(memory_space=pltpu.HBM),
            pl.BlockSpec(memory_space=pltpu.HBM),
            pl.BlockSpec(memory_space=pltpu.HBM),
            pl.BlockSpec(memory_space=smem),
            pl.BlockSpec(memory_space=smem),
        ],
        out_specs=pl.BlockSpec(memory_space=vmem),
        scratch_shapes=[
            vmem((64, 128, 128), f32),
            vmem((4, 4, 4, 128, 128), f32),
            vmem((4, 8), i32),
            vmem((8, 4, 64), i32),
            vmem((8, 128), i32),
            vmem((8, 8, 128), i32),
            vmem((8, 8, 128), i32),
            vmem((16, 8, 128), i32),
            smem((16, 8, 128), i32),
            smem((64,), i32),
            smem((64,), i32),
            smem((64,), f32),
            *[vmem((3, 4, 4, r, 128), f32) for r in rows],
            *[vmem((3, 4, r, 128), f32) for r in rows],
            *[vmem((3, r, 128), f32) for r in rows],
            *[vmem((4, 4, r, 128), f32) for r in rows],
            *[vmem((4, r, 128), f32) for r in rows],
            dma((4,)), dma((7,)), dma((7,)), dma((7,)), dma((8,)), dma((7,)), dma((8,)),
            dma((8,)), dma((8,)), dma((1,)), dma((1,)), dma((3, 9)), dma((3, 9)),
        ],
        compiler_params=pltpu.CompilerParams(
            collective_id=0, has_side_effects=True, vmem_limit_bytes=59 << 20),
        cost_estimate=pl.CostEstimate(flops=64 * 3 * 2 * 128**3, bytes_accessed=1 << 22, transcendentals=0),
        name="home_product",
    )(x_tiles, tile_col.T, keep_mask.transpose(0, 2, 1), out_rows, out_cols)


def solution(mesh):
    return jax.shard_map(
        per_device,
        mesh=mesh,
        in_specs=(
            P("inner", "cols", None, None),
            P("inner", "cols"),
            P("inner", None, "cols"),
            P(("inner", "cols")),
            P(("inner", "cols")),
        ),
        out_specs=P(("inner", "cols"), None, None),
        check_vma=False,
    )
```

time: 313 us -> 82.1 us (0.26)
  waiting for transfers between devices: 196 us -> 0 us
  Pallas kernels: 0 us -> 79.2 us
  matrix products: 55.5 us -> 0 us
  blocking collectives: 35.5 us -> 0 us
  between operations: 14.7 us -> 1.3 us
  local copies, waits for them, and re-layouts: 9.09 us -> 1.47 us
    all_gather x1 -> x0, waiting for transfers between devices: 126 us -> none  [per_device(): left = lax.all_gather(x_tiles, 'cols', axis=1, tiled=True)]
    pallas_call x0 -> x1, Pallas kernels: none -> 79.2 us  [per_device(): pl.pallas_call(kernel, out_shape=jax.ShapeDtypeStruct((1, 128, 128), f32)...]
    reduce_scatter x1 -> x0, waiting for transfers between devices: 69 us -> none  [per_device(): lax.psum_scatter(partial_value, 'inner', scatter_dimension=0, tiled=True)]
    dot_general x4 -> x0, matrix products: 55.5 us -> none  [the longest x1 37.4 us: per_device(): left_sum = jnp.einsum('mkp,kpab->mkab', pick_left, left, precision=high)]
    all_gather x1 -> x0, blocking collectives: 23.7 us -> none  [per_device(): left_cols = lax.all_gather(tile_col, 'cols', axis=1, tiled=True)]
    unnamed x1 -> x0, blocking collectives: 11.8 us -> none
    dot_general x2 -> x0, local copies, waits for them, and re-layouts: 5.51 us -> none  [the longest x1 5.38 us: per_device(): left_sum = jnp.einsum('mkp,kpab->mkab', pick_left, left, precision=high)]
  transfers between devices with their start and end apart: 2 -> 0, of which waited for: 2 -> 0; matrix products, arithmetic and copies ran while one was open for 4% -> 0% of each run, Pallas kernels for 0% -> 0%
where the time goes in v4:
time: 82.1 us; the launch traced here: 81.9 us
  Pallas kernels  79.2 us (96%)
  local copies, waits for them, and re-layouts  1.47 us (2%)
  between operations  1.3 us (2%)
    pallas_call x1, Pallas kernels, per_device(): pl.pallas_call(kernel, out_shape=jax.ShapeDtypeStruct((1, 128, 128), f32)...  79.2 us

profile of v4, /device:TPU:1, one launch (start us, length us, event | category | flops | bytes accessed | tf_op | source)
XLA Modules:
  0.0 81.9 jit_solution(15279859503471890151)
XLA Ops:
  1.3 79.2 %home_product.1 = f32[1,128,128]{2,1,0:T(8,128)} custom-call(f32[8,4,128,128]{3,2,1,0:T(8,128)} %x.1, s32[4,8]{1,0:T(4,128)} %bitcast.3, s32[8,4,64]{2,1,0:T(4,128)} %bitcast.2, s32[1]{0:T(128)S(6)} %copy.7.out_row, s32[1]{0:T(128)S(6)} %copy.8.out_col), custom_call_target="tpu_custom_call" | custom-call | flops 805306368 | bytes 4194304 | tf_op jit(solution)/shard_map/home_product/pallas_call | solution.py:231
  80.5 1.5 %copy.9 = f32[1,128,128]{2,1,0:T(8,128)} copy(f32[1,128,128]{2,1,0:T(8,128)} %home_product.1) | data formatting | bytes 131072

commit v5 on v4

v5 whole, which is shorter than its diff:
```python
import jax
import jax.numpy as jnp
from jax import lax
from jax.experimental import pallas as pl
from jax.experimental.pallas import tpu as pltpu
from jax.sharding import PartitionSpec as P

MESH = pl.DeviceIdType.MESH
JB_DEV = 60
PARTNERS = 16
STEPS = ((2, 1), (1, 1), (3, 1), (2, 0), (1, 0), (3, 0), (0, 1))
PARTS = ((0, 48, 24, (0, 1, 2)), (48, 40, 24, (1, 2, 0)), (88, 40, 24, (2, 0, 1)))


def kernel(x, tile_col_hbm, keep_hbm, out_row, out_col, out, held, left_top, left_low, right_top, right_low, products, tile_col, keep, mine, slots, notes, heard,
           heard_s, left_s, right_s, gate_s, via_a, via_b, via_c, one_a, one_b, one_c, two_a, two_b, two_c, three_a, three_b, three_c,
           sum_a, sum_b, sum_c, line_a, line_b, line_c,
           local_sem, own_sem, s_send, s_recv, n_send, n_recv, g_send, g_recv, c_send, c_recv, h_send, h_recv, f_send, f_recv,
           r_send, r_recv):
    i = lax.axis_index("inner")
    c = lax.axis_index("cols")
    core = c % 2
    at = (i // 2, c // 4, (i % 2) * 2 + (c // 2) % 2)
    z_hi, z_lo = i % 2, (c // 2) % 2
    home = at[1] * 2 + z_lo

    def device(place, on):
        px, py, pz = place
        return (px * 2 + pz // 2, py * 4 + (pz % 2) * 2 + on)

    def row_home(step):
        py, pz = (at[1] + step[0]) % 4, (z_lo + step[1]) % 2
        return py * 2 + pz, device((at[0], py, z_hi * 2 + pz), core)

    def inner(e):
        return ((i + e) % 8, c)

    def along(axis, d):
        return device(tuple((p + d) % 4 if n == axis else p for n, p in enumerate(at)), core)

    twin = device(at, 1 - core)

    def remote(src, dst, send, recv, to):
        return pltpu.make_async_remote_copy(
            src_ref=src, dst_ref=dst, send_sem=send, recv_sem=recv, device_id=to, device_id_type=MESH)

    load_col = pltpu.make_async_copy(tile_col_hbm, tile_col, local_sem.at[0])
    load_keep = pltpu.make_async_copy(keep_hbm, keep, local_sem.at[1])
    load_col.start()
    load_keep.start()

    def load_own(p):
        return pltpu.make_async_copy(x.at[home, p], held.at[p * 8 + home], own_sem.at[p])

    for p in range(4):
        load_own(p).start()

    barrier = pltpu.get_barrier_semaphore()
    partners = [row_home(step)[1] for step in STEPS] + [inner(e) for e in range(1, 8)]
    partners += [twin, device((at[0], at[1], 3 - at[2]), core)]
    for to in partners:
        pl.semaphore_signal(barrier, inc=1, device_id=to, device_id_type=MESH)

    sublane = lax.broadcasted_iota(jnp.int32, (8, 128), 0)
    lane = lax.broadcasted_iota(jnp.int32, (8, 128), 1)
    mine[...] = jnp.where(sublane == 4, out_row[0], jnp.where(sublane == 5, out_col[0], 0))
    slots[i] = mine[...]
    load_col.wait()
    load_keep.wait()
    pl.semaphore_wait(barrier, PARTNERS)

    slot_copies = [remote(mine, slots.at[i], s_send.at[e - 1], s_recv.at[e - 1], inner(e)) for e in range(1, 8)]
    for copy in slot_copies:
        copy.start()

    def send_blocks(p):
        for j, step in enumerate(STEPS):
            row, to = row_home(step)
            remote(x.at[row, p], held.at[p * 8 + home], g_send.at[j, p], g_recv.at[home, p], to).start()

    send_blocks(0)
    send_blocks(1)
    for copy in slot_copies:
        copy.wait_recv()

    listed = jnp.zeros((8, 128), jnp.int32)
    for s in range(8):
        listed = jnp.where(lane == s, slots[s], listed)
    for k in range(8):
        notes[k] = listed
        notes[k, 0:4, 0:64] = keep[k]
        notes[k, 0:4, 64:128] = jnp.broadcast_to(tile_col[:, k:k + 1], (4, 64))
    heard[home] = notes[home]

    def note(j):
        row, to = row_home(STEPS[j])
        return remote(notes.at[row], heard.at[home], n_send.at[j], n_recv.at[home], to)

    for j in range(7):
        note(j).start()
    send_blocks(2)
    send_blocks(3)

    def share(p):
        return remote(held.at[pl.ds(p * 8, 8)], held.at[pl.ds(32 + p * 8, 8)], c_send.at[p], c_recv.at[p], twin)

    def halves(v):
        top = v.astype(jnp.bfloat16)
        return top, (v - top.astype(jnp.float32)).astype(jnp.bfloat16)

    def prepare_left(n):
        left_top[n], left_low[n] = halves(held[n].T)

    def receive(p):
        for j, step in enumerate(STEPS):
            source, to = row_home(step)
            remote(x.at[0, p], held.at[p * 8 + source], g_send.at[j, p], g_recv.at[source, p], to).wait_recv()
        load_own(p).wait()
        share(p).start()

        def body(n, carry):
            for n in (p * 8 + 2 * n, p * 8 + 2 * n + 1):
                prepare_left(n)
                right_top[n], right_low[n] = halves(held[n])
            return carry

        lax.fori_loop(0, 4, body, 0)

    def receive_shared(p):
        share(p).wait_recv()

        def body(n, carry):
            for n in (p * 8 + 2 * n, p * 8 + 2 * n + 1):
                prepare_left(32 + n)
            return carry

        lax.fori_loop(0, 4, body, 0)

    receive(0)
    receive(1)
    receive_shared(0)
    for j, step in enumerate(STEPS):
        source, to = row_home(step)
        remote(notes.at[0], heard.at[source], n_send.at[j], n_recv.at[source], to).wait_recv()
    share_notes = remote(heard.at[pl.ds(0, 8)], heard.at[pl.ds(8, 8)], h_send.at[0], h_recv.at[0], twin)
    share_notes.start()
    receive_shared(1)
    share_notes.wait_recv()
    stage = pltpu.make_async_copy(heard, heard_s, local_sem.at[2])
    stage.start()
    receive(2)
    stage.wait()

    def find(n):
        sx, sy, sz = n // 16, (n // 4) % 4, n % 4
        index, chip = sx * 2 + sz // 2, sy * 2 + sz % 2
        row, col = heard_s[chip, 4, index], heard_s[chip, 5, index]
        left_slice = row // JB_DEV
        holder = jnp.where(left_slice % 2 == core, 0, 8) + left_slice // 2
        p, q, stored_l, stored_r = jnp.int32(0), jnp.int32(0), jnp.int32(0), jnp.int32(0)
        for r in range(4):
            hit = heard_s[holder, r, 64] == row
            p, stored_l = jnp.where(hit, r, p), jnp.where(hit, 1, stored_l)
            hit = heard_s[chip, r, 64] == col
            q, stored_r = jnp.where(hit, r, q), jnp.where(hit, 1, stored_r)
        left_s[n] = (holder // 8) * 32 + p * 8 + holder % 8
        right_s[n] = q * 8 + chip
        gate_s[n] = (heard_s[chip, q, left_slice * 4 + p] * stored_l * stored_r).astype(jnp.float32)

    def find_some(n, carry):
        for m in range(4):
            find(n * 4 + m)
        return carry

    lax.fori_loop(0, 16, find_some, 0)
    receive_shared(2)
    receive(3)
    receive_shared(3)

    def product(n):
        lt, ll, rt, rl = left_top[left_s[n]], left_low[left_s[n]], right_top[right_s[n]], right_low[right_s[n]]
        return gate_s[n] * (jnp.dot(lt, rt, preferred_element_type=jnp.float32)
                            + jnp.dot(lt, rl, preferred_element_type=jnp.float32)
                            + jnp.dot(ll, rt, preferred_element_type=jnp.float32))

    vias, ones, twos, threes = (via_a, via_b, via_c), (one_a, one_b, one_c), (two_a, two_b, two_c), (three_a, three_b, three_c)
    sums, lines = (sum_a, sum_b, sum_c), (line_a, line_b, line_c)

    def pick(axes_left, axis, where):
        return tuple(where if a == axis else slice(None) for a in axes_left)

    def first(part, way, kind):
        start, rows, split, (axis, _, _) = PARTS[part]
        ahead = 1 if way == 0 else 3
        low, high = (0, split), (split, rows - split)
        begin, count = (low if way == 0 else high) if kind != 1 else (high if way == 0 else low)
        if kind == 2:
            source = vias[part].at[way, :, :, pl.ds(begin, count)]
        else:
            cut = pick((0, 1, 2), axis, (at[axis] + (2 if kind == 0 else ahead)) % 4)
            source = products.at[cut + (pl.ds(start + begin, count),)]
        target = (vias if kind == 0 else ones)[part].at[way, :, :, pl.ds(begin, count)]
        n = way * 3 + kind
        return remote(source, target, f_send.at[part, n], f_recv.at[part, n], along(axis, ahead))

    def add_own(part, way):
        start, rows, split, (axis, _, _) = PARTS[part]
        first(part, way, 0).wait_recv()
        begin, count = (0, split) if way == 0 else (split, rows - split)

        def body(n, carry):
            cut = pick((0, 1, 2), axis, (at[axis] + 1 + 2 * way) % 4)
            one = [n if isinstance(a, slice) else a for a in cut]
            free = [j for j, a in enumerate(cut) if isinstance(a, slice)]
            one[free[0]], one[free[1]] = n // 4, n % 4
            rows_there = pl.ds(start + begin, count)
            here = (way, n // 4, n % 4, pl.ds(begin, count))
            vias[part][here] = vias[part][here] + products[tuple(one) + (rows_there,)]
            return carry

        lax.fori_loop(0, 16, body, 0)
        first(part, way, 2).start()

    def second(part, d):
        _, _, _, (gone, axis, _) = PARTS[part]
        cut = pick([a for a in range(3) if a != gone], axis, (at[axis] + d) % 4)
        return remote(sums[part].at[cut], twos[part].at[d - 1], r_send.at[part, d - 1], r_recv.at[part, d - 1], along(axis, d))

    def third(part, d):
        _, _, _, (_, _, axis) = PARTS[part]
        return remote(lines[part].at[(at[axis] + d) % 4], threes[part].at[d - 1],
                      r_send.at[part, 2 + d], r_recv.at[part, 2 + d], along(axis, d))

    def slab(j, carry):
        px = (at[0] + jnp.where(j < 2, 2 + j, 3 - j)) % 4

        def body(n, carry):
            for m in range(4):
                products[px, n, m] = product(px * 16 + n * 4 + m)
            return carry

        lax.fori_loop(0, 4, body, 0)

        @pl.when(j == 0)
        def _():
            first(0, 0, 0).start()
            first(0, 1, 0).start()

        @pl.when(j == 1)
        def _():
            first(0, 1, 1).start()

        @pl.when(j == 2)
        def _():
            first(0, 0, 1).start()

        return carry

    lax.fori_loop(0, 4, slab, 0)
    for kind in range(2):
        for part in (1, 2):
            for way in range(2):
                first(part, way, kind).start()
    for part in range(3):
        for way in range(2):
            add_own(part, way)

    for part, (start, rows, _, (axis, _, _)) in enumerate(PARTS):
        for way in range(2):
            first(part, way, 1).wait_recv()
            first(part, way, 2).wait_recv()

        def total(n, carry):
            cut = pick((0, 1, 2), axis, at[axis])
            one, free = list(cut), [j for j, a in enumerate(cut) if isinstance(a, slice)]
            one[free[0]], one[free[1]] = n // 4, n % 4
            sums[part][n // 4, n % 4] = (products[tuple(one) + (pl.ds(start, rows),)]
                                         + ones[part][0, n // 4, n % 4] + ones[part][1, n // 4, n % 4])
            return carry

        lax.fori_loop(0, 16, total, 0)
        for d in (2, 1, 3):
            second(part, d).start()
    for part, (_, _, _, (gone, axis, _)) in enumerate(PARTS):
        for d in range(1, 4):
            second(part, d).wait_recv()
        cut = pick([a for a in range(3) if a != gone], axis, at[axis])
        lines[part][...] = sums[part][cut] + twos[part][0] + twos[part][1] + twos[part][2]
        for d in (2, 1, 3):
            third(part, d).start()
    for part, (start, rows, _, (_, _, axis)) in enumerate(PARTS):
        for d in range(1, 4):
            third(part, d).wait_recv()
        out[0, pl.ds(start, rows)] = lines[part][at[axis]] + threes[part][0] + threes[part][1] + threes[part][2]

    for copy in slot_copies + [share_notes]:
        copy.wait_send()
    for j, step in enumerate(STEPS):
        note(j).wait_send()
        row, to = row_home(step)
        for p in range(4):
            remote(x.at[row, p], held.at[p * 8 + home], g_send.at[j, p], g_recv.at[home, p], to).wait_send()
    for p in range(4):
        share(p).wait_send()
    for part in range(3):
        for d in range(1, 4):
            second(part, d).wait_send()
            third(part, d).wait_send()
        for way in range(2):
            for kind in range(3):
                first(part, way, kind).wait_send()


def per_device(x_tiles, tile_col, keep_mask, out_rows, out_cols):
    vmem, smem = pltpu.VMEM, pltpu.SMEM
    dma = pltpu.SemaphoreType.DMA
    f32, i32 = jnp.float32, jnp.int32
    rows = [part[1] for part in PARTS]
    return pl.pallas_call(
        kernel,
        out_shape=jax.ShapeDtypeStruct((1, 128, 128), f32),
        in_specs=[
            pl.BlockSpec(memory_space=pltpu.HBM),
            pl.BlockSpec(memory_space=pltpu.HBM),
            pl.BlockSpec(memory_space=pltpu.HBM),
            pl.BlockSpec(memory_space=smem),
            pl.BlockSpec(memory_space=smem),
        ],
        out_specs=pl.BlockSpec(memory_space=vmem),
        scratch_shapes=[
            vmem((64, 128, 128), f32),
            vmem((64, 128, 128), jnp.bfloat16),
            vmem((64, 128, 128), jnp.bfloat16),
            vmem((32, 128, 128), jnp.bfloat16),
            vmem((32, 128, 128), jnp.bfloat16),
            vmem((4, 4, 4, 128, 128), f32),
            vmem((4, 8), i32),
            vmem((8, 4, 64), i32),
            vmem((8, 128), i32),
            vmem((8, 8, 128), i32),
            vmem((8, 8, 128), i32),
            vmem((16, 8, 128), i32),
            smem((16, 8, 128), i32),
            smem((64,), i32),
            smem((64,), i32),
            smem((64,), f32),
            *[vmem((2, 4, 4, r, 128), f32) for r in rows],
            *[vmem((2, 4, 4, r, 128), f32) for r in rows],
            *[vmem((3, 4, r, 128), f32) for r in rows],
            *[vmem((3, r, 128), f32) for r in rows],
            *[vmem((4, 4, r, 128), f32) for r in rows],
            *[vmem((4, r, 128), f32) for r in rows],
            dma((3,)), dma((4,)), dma((7,)), dma((7,)), dma((7,)), dma((8,)), dma((7, 4)), dma((8, 4)),
            dma((4,)), dma((4,)), dma((1,)), dma((1,)), dma((3, 6)), dma((3, 6)), dma((3, 6)), dma((3, 6)),
        ],
        compiler_params=pltpu.CompilerParams(
            collective_id=0, has_side_effects=True, vmem_limit_bytes=59 << 20),
        cost_estimate=pl.CostEstimate(flops=64 * 3 * 2 * 128**3, bytes_accessed=1 << 22, transcendentals=0),
        name="home_product",
    )(x_tiles, tile_col.T, keep_mask.transpose(0, 2, 1), out_rows, out_cols)


def solution(mesh):
    return jax.shard_map(
        per_device,
        mesh=mesh,
        in_specs=(
            P("inner", "cols", None, None),
            P("inner", "cols"),
            P("inner", None, "cols"),
            P(("inner", "cols")),
            P(("inner", "cols")),
        ),
        out_specs=P(("inner", "cols"), None, None),
        check_vma=False,
    )
```

time: 82.1 us -> 70.8 us (0.86)
  Pallas kernels: 79.2 us -> 67.8 us
    pallas_call x1, Pallas kernels: 79.2 us -> 67.8 us  [per_device(): pl.pallas_call(kernel, out_shape=jax.ShapeDtypeStruct((1, 128, 128), f32)...]
where the time goes in v5:
time: 70.8 us; the launch traced here: 70.6 us
  Pallas kernels  67.8 us (96%)
  local copies, waits for them, and re-layouts  1.47 us (2%)
  between operations  1.3 us (2%)
    pallas_call x1, Pallas kernels, per_device(): pl.pallas_call(kernel, out_shape=jax.ShapeDtypeStruct((1, 128, 128), f32)...  67.8 us
    unnamed x1, local copies, waits for them, and re-layouts  1.47 us

profile of v5, /device:TPU:1, one launch (start us, length us, event | category | flops | bytes accessed | tf_op | source)
XLA Modules:
  0.0 70.6 jit_solution(10476516334910808348)
XLA Ops:
  1.3 67.8 %home_product.1 = f32[1,128,128]{2,1,0:T(8,128)} custom-call(f32[8,4,128,128]{3,2,1,0:T(8,128)} %x.1, s32[4,8]{1,0:T(4,128)} %bitcast.3, s32[8,4,64]{2,1,0:T(4,128)} %bitcast.2, s32[1]{0:T(128)S(6)} %copy.7.out_row, s32[1]{0:T(128)S(6)} %copy.8.out_col), custom_call_target="tpu_custom_call" | custom-call | flops 805306368 | bytes 4194304 | tf_op jit(solution)/shard_map/home_product/pallas_call | solution.py:319
  69.1 1.5 %copy.9 = f32[1,128,128]{2,1,0:T(8,128)} copy(f32[1,128,128]{2,1,0:T(8,128)} %home_product.1) | data formatting | bytes 131072

commit v6 on v5

--- a/solution.py
+++ b/solution.py
@@ -9,14 +9,18 @@
 JB_DEV = 60
 PARTNERS = 16
 STEPS = ((2, 1), (1, 1), (3, 1), (2, 0), (1, 0), (3, 0), (0, 1))
-PARTS = ((0, 48, 24, (0, 1, 2)), (48, 40, 24, (1, 2, 0)), (88, 40, 24, (2, 0, 1)))
-
-
-def kernel(x, tile_col_hbm, keep_hbm, out_row, out_col, out, held, left_top, left_low, right_top, right_low, products, tile_col, keep, mine, slots, notes, heard,
-           heard_s, left_s, right_s, gate_s, via_a, via_b, via_c, one_a, one_b, one_c, two_a, two_b, two_c, three_a, three_b, three_c,
-           sum_a, sum_b, sum_c, line_a, line_b, line_c,
-           local_sem, own_sem, s_send, s_recv, n_send, n_recv, g_send, g_recv, c_send, c_recv, h_send, h_recv, f_send, f_recv,
-           r_send, r_recv):
+PARTS = (
+    (0, 24, 16, (0, 1, 2)), (48, 24, 16, (1, 2, 0)), (88, 24, 16, (2, 0, 1)),
+    (24, 24, 8, (0, 1, 2)), (72, 16, 8, (1, 2, 0)), (112, 16, 8, (2, 0, 1)),
+)
+HALVES = ((0, 1, 2), (3, 4, 5))
+
+
+def kernel(x, tile_col_hbm, keep_hbm, out_row, out_col, out, held, left_top, left_low, right_top, right_low, products,
+           tile_col, keep, mine, slots, notes, heard, heard_s, left_s, right_s, gate_s, *rest):
+    vias, ones, twos, threes, sums, lines = (rest[6 * n:6 * n + 6] for n in range(6))
+    (local_sem, own_sem, s_send, s_recv, n_send, n_recv, g_send, g_recv, c_send, c_recv, h_send, h_recv,
+     f_send, f_recv, r_send, r_recv) = rest[36:]
     i = lax.axis_index("inner")
     c = lax.axis_index("cols")
     core = c % 2
@@ -183,9 +187,6 @@
                             + jnp.dot(lt, rl, preferred_element_type=jnp.float32)
                             + jnp.dot(ll, rt, preferred_element_type=jnp.float32))
 
-    vias, ones, twos, threes = (via_a, via_b, via_c), (one_a, one_b, one_c), (two_a, two_b, two_c), (three_a, three_b, three_c)
-    sums, lines = (sum_a, sum_b, sum_c), (line_a, line_b, line_c)
-
     def pick(axes_left, axis, where):
         return tuple(where if a == axis else slice(None) for a in axes_left)
 
@@ -208,17 +209,17 @@
         first(part, way, 0).wait_recv()
         begin, count = (0, split) if way == 0 else (split, rows - split)
 
+        cut = pick((0, 1, 2), axis, (at[axis] + 1 + 2 * way) % 4)
+        free = [j for j, a in enumerate(cut) if isinstance(a, slice)]
+
         def body(n, carry):
-            cut = pick((0, 1, 2), axis, (at[axis] + 1 + 2 * way) % 4)
-            one = [n if isinstance(a, slice) else a for a in cut]
-            free = [j for j, a in enumerate(cut) if isinstance(a, slice)]
-            one[free[0]], one[free[1]] = n // 4, n % 4
-            rows_there = pl.ds(start + begin, count)
-            here = (way, n // 4, n % 4, pl.ds(begin, count))
-            vias[part][here] = vias[part][here] + products[tuple(one) + (rows_there,)]
-            return carry
-
-        lax.fori_loop(0, 16, body, 0)
+            one = list(cut)
+            one[free[0]] = n
+            here = (way, n, slice(None), pl.ds(begin, count))
+            vias[part][here] = vias[part][here] + products[tuple(one) + (pl.ds(start + begin, count),)]
+            return carry
+
+        lax.fori_loop(0, 4, body, 0)
         first(part, way, 2).start()
 
     def second(part, d):
@@ -235,11 +236,11 @@
         px = (at[0] + jnp.where(j < 2, 2 + j, 3 - j)) % 4
 
         def body(n, carry):
-            for m in range(4):
-                products[px, n, m] = product(px * 16 + n * 4 + m)
-            return carry
-
-        lax.fori_loop(0, 4, body, 0)
+            for m in range(8):
+                products[px, 2 * n + m // 4, m % 4] = product(px * 16 + n * 8 + m)
+            return carry
+
+        lax.fori_loop(0, 2, body, 0)
 
         @pl.when(j == 0)
         def _():
@@ -257,11 +258,18 @@
         return carry
 
     lax.fori_loop(0, 4, slab, 0)
-    for kind in range(2):
-        for part in (1, 2):
-            for way in range(2):
-                first(part, way, kind).start()
-    for part in range(3):
+    def both_ways(part, kind):
+        for way in range(2):
+            first(part, way, kind).start()
+
+    for part, kind in ((1, 0), (2, 0), (1, 1), (2, 1), (3, 0), (4, 0), (5, 0)):
+        both_ways(part, kind)
+    for part in HALVES[0]:
+        for way in range(2):
+            add_own(part, way)
+    for part in HALVES[1]:
+        both_ways(part, 1)
+    for part in HALVES[1]:
         for way in range(2):
             add_own(part, way)
 
@@ -270,15 +278,16 @@
             first(part, way, 1).wait_recv()
             first(part, way, 2).wait_recv()
 
+        cut = pick((0, 1, 2), axis, at[axis])
+        free = [j for j, a in enumerate(cut) if isinstance(a, slice)]
+
         def total(n, carry):
-            cut = pick((0, 1, 2), axis, at[axis])
-            one, free = list(cut), [j for j, a in enumerate(cut) if isinstance(a, slice)]
-            one[free[0]], one[free[1]] = n // 4, n % 4
-            sums[part][n // 4, n % 4] = (products[tuple(one) + (pl.ds(start, rows),)]
-                                         + ones[part][0, n // 4, n % 4] + ones[part][1, n // 4, n % 4])
-            return carry
-
-        lax.fori_loop(0, 16, total, 0)
+            one = list(cut)
+            one[free[0]] = n
+            sums[part][n] = products[tuple(one) + (pl.ds(start, rows),)] + ones[part][0, n] + ones[part][1, n]
+            return carry
+
+        lax.fori_loop(0, 4, total, 0)
         for d in (2, 1, 3):
             second(part, d).start()
     for part, (_, _, _, (gone, axis, _)) in enumerate(PARTS):
@@ -302,7 +311,7 @@
             remote(x.at[row, p], held.at[p * 8 + home], g_send.at[j, p], g_recv.at[home, p], to).wait_send()
     for p in range(4):
         share(p).wait_send()
-    for part in range(3):
+    for part in range(6):
         for d in range(1, 4):
             second(part, d).wait_send()
             third(part, d).wait_send()
@@ -351,13 +360,13 @@
             *[vmem((4, 4, r, 128), f32) for r in rows],
             *[vmem((4, r, 128), f32) for r in rows],
             dma((3,)), dma((4,)), dma((7,)), dma((7,)), dma((7,)), dma((8,)), dma((7, 4)), dma((8, 4)),
-            dma((4,)), dma((4,)), dma((1,)), dma((1,)), dma((3, 6)), dma((3, 6)), dma((3, 6)), dma((3, 6)),
+            dma((4,)), dma((4,)), dma((1,)), dma((1,)), dma((6, 6)), dma((6, 6)), dma((6, 6)), dma((6, 6)),
         ],
         compiler_params=pltpu.CompilerParams(
-            collective_id=0, has_side_effects=True, vmem_limit_bytes=59 << 20),
+            collective_id=0, has_side_effects=True, vmem_limit_bytes=40 << 20),
         cost_estimate=pl.CostEstimate(flops=64 * 3 * 2 * 128**3, bytes_accessed=1 << 22, transcendentals=0),
         name="home_product",
-    )(x_tiles, tile_col.T, keep_mask.transpose(0, 2, 1), out_rows, out_cols)
+    )(*(pltpu.with_memory_space_constraint(a, pltpu.HBM) for a in (x_tiles, tile_col.T, keep_mask.transpose(0, 2, 1))), out_rows, out_cols)
 
 
 def solution(mesh):

time: 70.8 us -> 67.1 us (0.948)
  Pallas kernels: 67.8 us -> 65 us
  local copies, waits for them, and re-layouts: 1.47 us -> 0.63 us
    pallas_call x1, Pallas kernels: 67.8 us -> 65 us  [per_device(): pl.pallas_call(kernel, out_shape=jax.ShapeDtypeStruct((1, 128, 128), f32)...]
    unnamed x1, local copies, waits for them, and re-layouts: 1.47 us -> 0.63 us
where the time goes in v6:
time: 67.1 us; the launch traced here: 66.9 us
  Pallas kernels  65 us (97%)
  between operations  1.3 us (2%)
    pallas_call x1, Pallas kernels, per_device(): pl.pallas_call(kernel, out_shape=jax.ShapeDtypeStruct((1, 128, 128), f32)...  65 us

profile of v6, /device:TPU:1, one launch (start us, length us, event | category | flops | bytes accessed | tf_op | source)
XLA Modules:
  0.0 66.9 jit_solution(11112070562357487828)
XLA Ops:
  1.3 65.0 %home_product.1 = f32[1,128,128]{2,1,0:T(8,128)S(1)} custom-call(f32[8,4,128,128]{3,2,1,0:T(8,128)} %x.1, s32[4,8]{1,0:T(4,128)} %bitcast.3, s32[8,4,64]{2,1,0:T(4,128)} %bitcast.2, s32[1]{0:T(128)S(6)} %copy.7.out_row, s32[1]{0:T(128)S(6)} %copy.8.out_col), custom_call_target="tpu_custom_call" | custom-call | flops 805306368 | bytes 4194304 | tf_op jit(solution)/shard_map/home_product/pallas_call | solution.py:328
  66.3 0.6 copy.9

commit v7 on v6

--- a/solution.py
+++ b/solution.py
@@ -8,19 +8,17 @@
 MESH = pl.DeviceIdType.MESH
 JB_DEV = 60
 PARTNERS = 16
-STEPS = ((2, 1), (1, 1), (3, 1), (2, 0), (1, 0), (3, 0), (0, 1))
-PARTS = (
-    (0, 24, 16, (0, 1, 2)), (48, 24, 16, (1, 2, 0)), (88, 24, 16, (2, 0, 1)),
-    (24, 24, 8, (0, 1, 2)), (72, 16, 8, (1, 2, 0)), (112, 16, 8, (2, 0, 1)),
-)
+STEPS = ((0, 1), (1, 0), (3, 0), (1, 1), (3, 1), (2, 0), (2, 1))
+PARTS = ((0, 32, 16, (0, 1, 2)), (48, 24, 16, (1, 2, 0)), (88, 24, 8, (2, 0, 1)), (32, 16, 8, (0, 1, 2)), (72, 16, 8, (1, 2, 0)), (112, 16, 8, (2, 0, 1)))
 HALVES = ((0, 1, 2), (3, 4, 5))
 
 
 def kernel(x, tile_col_hbm, keep_hbm, out_row, out_col, out, held, left_top, left_low, right_top, right_low, products,
            tile_col, keep, mine, slots, notes, heard, heard_s, left_s, right_s, gate_s, *rest):
-    vias, ones, twos, threes, sums, lines = (rest[6 * n:6 * n + 6] for n in range(6))
+    vias, ones, twos, sums = (rest[6 * n:6 * n + 6] for n in range(4))
+    threes, lines = rest[24:27], rest[27:30]
     (local_sem, own_sem, s_send, s_recv, n_send, n_recv, g_send, g_recv, c_send, c_recv, h_send, h_recv,
-     f_send, f_recv, r_send, r_recv) = rest[36:]
+     f_send, f_recv, r_send, r_recv) = rest[30:]
     i = lax.axis_index("inner")
     c = lax.axis_index("cols")
     core = c % 2
@@ -74,15 +72,14 @@
     pl.semaphore_wait(barrier, PARTNERS)
 
     slot_copies = [remote(mine, slots.at[i], s_send.at[e - 1], s_recv.at[e - 1], inner(e)) for e in range(1, 8)]
-    for copy in slot_copies:
-        copy.start()
-
     def send_blocks(p):
         for j, step in enumerate(STEPS):
             row, to = row_home(step)
             remote(x.at[row, p], held.at[p * 8 + home], g_send.at[j, p], g_recv.at[home, p], to).start()
 
     send_blocks(0)
+    for copy in slot_copies:
+        copy.start()
     send_blocks(1)
     for copy in slot_copies:
         copy.wait_recv()
@@ -122,23 +119,15 @@
         load_own(p).wait()
         share(p).start()
 
-        def body(n, carry):
-            for n in (p * 8 + 2 * n, p * 8 + 2 * n + 1):
-                prepare_left(n)
-                right_top[n], right_low[n] = halves(held[n])
-            return carry
-
-        lax.fori_loop(0, 4, body, 0)
+        for n in range(p * 8, p * 8 + 8):
+            prepare_left(n)
+            right_top[n], right_low[n] = halves(held[n])
 
     def receive_shared(p):
         share(p).wait_recv()
 
-        def body(n, carry):
-            for n in (p * 8 + 2 * n, p * 8 + 2 * n + 1):
-                prepare_left(32 + n)
-            return carry
-
-        lax.fori_loop(0, 4, body, 0)
+        for n in range(p * 8, p * 8 + 8):
+            prepare_left(32 + n)
 
     receive(0)
     receive(1)
@@ -152,7 +141,6 @@
     share_notes.wait_recv()
     stage = pltpu.make_async_copy(heard, heard_s, local_sem.at[2])
     stage.start()
-    receive(2)
     stage.wait()
 
     def find(n):
@@ -177,6 +165,7 @@
         return carry
 
     lax.fori_loop(0, 16, find_some, 0)
+    receive(2)
     receive_shared(2)
     receive(3)
     receive_shared(3)
@@ -227,20 +216,16 @@
         cut = pick([a for a in range(3) if a != gone], axis, (at[axis] + d) % 4)
         return remote(sums[part].at[cut], twos[part].at[d - 1], r_send.at[part, d - 1], r_recv.at[part, d - 1], along(axis, d))
 
-    def third(part, d):
-        _, _, _, (_, _, axis) = PARTS[part]
-        return remote(lines[part].at[(at[axis] + d) % 4], threes[part].at[d - 1],
-                      r_send.at[part, 2 + d], r_recv.at[part, 2 + d], along(axis, d))
+    def third(order, d):
+        axis = PARTS[order][3][2]
+        return remote(lines[order].at[(at[axis] + d) % 4], threes[order].at[d - 1],
+                      r_send.at[order, 2 + d], r_recv.at[order, 2 + d], along(axis, d))
 
     def slab(j, carry):
         px = (at[0] + jnp.where(j < 2, 2 + j, 3 - j)) % 4
 
-        def body(n, carry):
-            for m in range(8):
-                products[px, 2 * n + m // 4, m % 4] = product(px * 16 + n * 8 + m)
-            return carry
-
-        lax.fori_loop(0, 2, body, 0)
+        for m in range(16):
+            products[px, m // 4, m % 4] = product(px * 16 + m)
 
         @pl.when(j == 0)
         def _():
@@ -264,44 +249,6 @@
 
     for part, kind in ((1, 0), (2, 0), (1, 1), (2, 1), (3, 0), (4, 0), (5, 0)):
         both_ways(part, kind)
-    for part in HALVES[0]:
-        for way in range(2):
-            add_own(part, way)
-    for part in HALVES[1]:
-        both_ways(part, 1)
-    for part in HALVES[1]:
-        for way in range(2):
-            add_own(part, way)
-
-    for part, (start, rows, _, (axis, _, _)) in enumerate(PARTS):
-        for way in range(2):
-            first(part, way, 1).wait_recv()
-            first(part, way, 2).wait_recv()
-
-        cut = pick((0, 1, 2), axis, at[axis])
-        free = [j for j, a in enumerate(cut) if isinstance(a, slice)]
-
-        def total(n, carry):
-            one = list(cut)
-            one[free[0]] = n
-            sums[part][n] = products[tuple(one) + (pl.ds(start, rows),)] + ones[part][0, n] + ones[part][1, n]
-            return carry
-
-        lax.fori_loop(0, 4, total, 0)
-        for d in (2, 1, 3):
-            second(part, d).start()
-    for part, (_, _, _, (gone, axis, _)) in enumerate(PARTS):
-        for d in range(1, 4):
-            second(part, d).wait_recv()
-        cut = pick([a for a in range(3) if a != gone], axis, at[axis])
-        lines[part][...] = sums[part][cut] + twos[part][0] + twos[part][1] + twos[part][2]
-        for d in (2, 1, 3):
-            third(part, d).start()
-    for part, (start, rows, _, (_, _, axis)) in enumerate(PARTS):
-        for d in range(1, 4):
-            third(part, d).wait_recv()
-        out[0, pl.ds(start, rows)] = lines[part][at[axis]] + threes[part][0] + threes[part][1] + threes[part][2]
-
     for copy in slot_copies + [share_notes]:
         copy.wait_send()
     for j, step in enumerate(STEPS):
@@ -311,13 +258,58 @@
             remote(x.at[row, p], held.at[p * 8 + home], g_send.at[j, p], g_recv.at[home, p], to).wait_send()
     for p in range(4):
         share(p).wait_send()
+    for part in HALVES[0]:
+        for way in range(2):
+            add_own(part, way)
+    for part in HALVES[1]:
+        both_ways(part, 1)
+    for part in HALVES[1]:
+        for way in range(2):
+            add_own(part, way)
+
+    for part, (start, rows, _, (axis, _, _)) in enumerate(PARTS):
+        for way in range(2):
+            first(part, way, 1).wait_recv()
+            first(part, way, 2).wait_recv()
+
+        cut = pick((0, 1, 2), axis, at[axis])
+        free = [j for j, a in enumerate(cut) if isinstance(a, slice)]
+
+        def total(n, carry):
+            one = list(cut)
+            one[free[0]] = n
+            sums[part][n] = products[tuple(one) + (pl.ds(start, rows),)] + ones[part][0, n] + ones[part][1, n]
+            return carry
+
+        lax.fori_loop(0, 4, total, 0)
+        for d in (2, 1, 3):
+            second(part, d).start()
+    for part in range(6):
+        for way in range(2):
+            for kind in range(3):
+                first(part, way, kind).wait_send()
+    for part in (0, 3, 1, 4, 2, 5):
+        _, rows, _, (gone, axis, _) = PARTS[part]
+        order, inside = part % 3, (PARTS[part][0] - PARTS[part % 3][0])
+        for d in range(1, 4):
+            second(part, d).wait_recv()
+        cut = pick([a for a in range(3) if a != gone], axis, at[axis])
+        lines[order][:, pl.ds(inside, rows)] = sums[part][cut] + twos[part][0] + twos[part][1] + twos[part][2]
+        if part > 2:
+            for d in (2, 1, 3):
+                third(order, d).start()
     for part in range(6):
         for d in range(1, 4):
             second(part, d).wait_send()
-            third(part, d).wait_send()
-        for way in range(2):
-            for kind in range(3):
-                first(part, way, kind).wait_send()
+    for order in range(3):
+        start, rows, axis = PARTS[order][0], PARTS[order][1] + PARTS[order + 3][1], PARTS[order][3][2]
+        for d in range(1, 4):
+            third(order, d).wait_recv()
+        out[0, pl.ds(start, rows)] = lines[order][at[axis]] + threes[order][0] + threes[order][1] + threes[order][2]
+
+    for order in range(3):
+        for d in range(1, 4):
+            third(order, d).wait_send()
 
 
 def per_device(x_tiles, tile_col, keep_mask, out_rows, out_cols):
@@ -356,9 +348,9 @@
             *[vmem((2, 4, 4, r, 128), f32) for r in rows],
             *[vmem((2, 4, 4, r, 128), f32) for r in rows],
             *[vmem((3, 4, r, 128), f32) for r in rows],
-            *[vmem((3, r, 128), f32) for r in rows],
             *[vmem((4, 4, r, 128), f32) for r in rows],
-            *[vmem((4, r, 128), f32) for r in rows],
+            *[vmem((3, rows[n] + rows[n + 3], 128), f32) for n in range(3)],
+            *[vmem((4, rows[n] + rows[n + 3], 128), f32) for n in range(3)],
             dma((3,)), dma((4,)), dma((7,)), dma((7,)), dma((7,)), dma((8,)), dma((7, 4)), dma((8, 4)),
             dma((4,)), dma((4,)), dma((1,)), dma((1,)), dma((6, 6)), dma((6, 6)), dma((6, 6)), dma((6, 6)),
         ],

time: 67.1 us -> 63.5 us (0.946)
  Pallas kernels: 65 us -> 61.4 us
    pallas_call x1, Pallas kernels: 65 us -> 61.4 us  [per_device(): pl.pallas_call(kernel, out_shape=jax.ShapeDtypeStruct((1, 128, 128), f32)...]
where the time goes in v7:
time: 63.5 us; the launch traced here: 63.3 us
  Pallas kernels  61.4 us (97%)
  between operations  1.3 us (2%)
    pallas_call x1, Pallas kernels, per_device(): pl.pallas_call(kernel, out_shape=jax.ShapeDtypeStruct((1, 128, 128), f32)...  61.4 us

profile of v7, /device:TPU:1, one launch (start us, length us, event | category | flops | bytes accessed | tf_op | source)
XLA Modules:
  0.0 63.3 jit_solution(7155894861111596748)
XLA Ops:
  1.3 61.4 %home_product.1 = f32[1,128,128]{2,1,0:T(8,128)S(1)} custom-call(f32[8,4,128,128]{3,2,1,0:T(8,128)} %x.1, s32[4,8]{1,0:T(4,128)} %bitcast.3, s32[8,4,64]{2,1,0:T(4,128)} %bitcast.2, s32[1]{0:T(128)S(6)} %copy.7.out_row, s32[1]{0:T(128)S(6)} %copy.8.out_col), custom_call_target="tpu_custom_call" | custom-call | flops 805306368 | bytes 4194304 | tf_op jit(solution)/shard_map/home_product/pallas_call | solution.py:320
  62.7 0.6 copy.9

commit v8 on v7

--- a/solution.py
+++ b/solution.py
@@ -9,7 +9,7 @@
 JB_DEV = 60
 PARTNERS = 16
 STEPS = ((0, 1), (1, 0), (3, 0), (1, 1), (3, 1), (2, 0), (2, 1))
-PARTS = ((0, 32, 16, (0, 1, 2)), (48, 24, 16, (1, 2, 0)), (88, 24, 8, (2, 0, 1)), (32, 16, 8, (0, 1, 2)), (72, 16, 8, (1, 2, 0)), (112, 16, 8, (2, 0, 1)))
+PARTS = ((0, 24, 16, (0, 1, 2)), (48, 24, 16, (1, 2, 0)), (88, 24, 16, (2, 0, 1)), (24, 24, 8, (0, 1, 2)), (72, 16, 8, (1, 2, 0)), (112, 16, 8, (2, 0, 1)))
 HALVES = ((0, 1, 2), (3, 4, 5))
 
 
@@ -229,8 +229,9 @@
 
         @pl.when(j == 0)
         def _():
-            first(0, 0, 0).start()
-            first(0, 1, 0).start()
+            for part in (0, 3):
+                first(part, 0, 0).start()
+                first(part, 1, 0).start()
 
         @pl.when(j == 1)
         def _():
@@ -247,7 +248,7 @@
         for way in range(2):
             first(part, way, kind).start()
 
-    for part, kind in ((1, 0), (2, 0), (1, 1), (2, 1), (3, 0), (4, 0), (5, 0)):
+    for part, kind in ((1, 0), (2, 0), (1, 1), (2, 1), (4, 0), (5, 0)):
         both_ways(part, kind)
     for copy in slot_copies + [share_notes]:
         copy.wait_send()

time: 63.5 us -> 63.4 us (level)
  no operation moved by 1% of the time
where the time goes in v8:
time: 63.4 us; the launch traced here: 63.2 us
  Pallas kernels  61.3 us (97%)
  between operations  1.3 us (2%)
    pallas_call x1, Pallas kernels, per_device(): pl.pallas_call(kernel, out_shape=jax.ShapeDtypeStruct((1, 128, 128), f32)...  61.3 us

profile of v8, /device:TPU:1, one launch (start us, length us, event | category | flops | bytes accessed | tf_op | source)
XLA Modules:
  0.0 63.2 jit_solution(4094389105608021984)
XLA Ops:
  1.3 61.3 %home_product.1 = f32[1,128,128]{2,1,0:T(8,128)S(1)} custom-call(f32[8,4,128,128]{3,2,1,0:T(8,128)} %x.1, s32[4,8]{1,0:T(4,128)} %bitcast.3, s32[8,4,64]{2,1,0:T(4,128)} %bitcast.2, s32[1]{0:T(128)S(6)} %copy.7.out_row, s32[1]{0:T(128)S(6)} %copy.8.out_col), custom_call_target="tpu_custom_call" | custom-call | flops 805306368 | bytes 4194304 | tf_op jit(solution)/shard_map/home_product/pallas_call | solution.py:321
  62.6 0.6 copy.9

commit v9 on v8

--- a/solution.py
+++ b/solution.py
@@ -289,7 +289,7 @@
         for way in range(2):
             for kind in range(3):
                 first(part, way, kind).wait_send()
-    for part in (0, 3, 1, 4, 2, 5):
+    for part in range(6):
         _, rows, _, (gone, axis, _) = PARTS[part]
         order, inside = part % 3, (PARTS[part][0] - PARTS[part % 3][0])
         for d in range(1, 4):

time: 63.4 us -> 63.4 us (level)
  no operation moved by 1% of the time
where the time goes in v9:
time: 63.4 us; the launch traced here: 63.2 us
  Pallas kernels  61.3 us (97%)
  between operations  1.3 us (2%)
    pallas_call x1, Pallas kernels, per_device(): pl.pallas_call(kernel, out_shape=jax.ShapeDtypeStruct((1, 128, 128), f32)...  61.3 us

profile of v9, /device:TPU:1, one launch (start us, length us, event | category | flops | bytes accessed | tf_op | source)
XLA Modules:
  0.0 63.2 jit_solution(17947030966123374500)
XLA Ops:
  1.3 61.3 %home_product.1 = f32[1,128,128]{2,1,0:T(8,128)S(1)} custom-call(f32[8,4,128,128]{3,2,1,0:T(8,128)} %x.1, s32[4,8]{1,0:T(4,128)} %bitcast.3, s32[8,4,64]{2,1,0:T(4,128)} %bitcast.2, s32[1]{0:T(128)S(6)} %copy.7.out_row, s32[1]{0:T(128)S(6)} %copy.8.out_col), custom_call_target="tpu_custom_call" | custom-call | flops 805306368 | bytes 4194304 | tf_op jit(solution)/shard_map/home_product/pallas_call | solution.py:321
  62.6 0.6 %copy.9 = f32[1,128,128]{2,1,0:T(8,128)} copy(f32[1,128,128]{2,1,0:T(8,128)S(1)} %home_product.1) | data formatting | bytes 131072
